TPU v7x, 32 devices: a whole 2x2x4 slice. The times are simulated.
32 devices in a mesh: dom: 8 (over y, x, core), cls: 4 (over z).
Axes of the slice: x: 2, y: 2, z: 4, core: 2. Of those that a mesh axis runs over, the one named last changes fastest.
Arguments:
- particles: bfloat16 [512, 16384], P(('dom', 'cls')), may hold values from -6 to 6
- averages: float32 [128, 16384], P('cls'), may hold values from -4 to 4
- prior_mass: float32 [128], P('cls'), may hold values from 1 to 8
- group_ids: int32 [4, 512, 1], P(None, ('dom', 'cls')), may hold values from 0 to 3; in each aligned block of 16 rows (0 to 15, 16 to 31, ..., all dimensions but the last counted through in order) at most 6 rows name the same one
- class_ids: int32 [4, 512], P(None, ('dom', 'cls')), may hold values from 0 to 31
- rot_ids: int32 [4, 512], P(None, ('dom', 'cls')), may hold values from 0 to 63
- weights: bfloat16 [4, 512], P(None, ('dom', 'cls')), may hold values from 0.25 to 4
- owners: int32 [4], replicated, may hold values from 0 to 3
Outputs:
- scores: float32 [4, 512, 2048], P(None, ('dom', 'cls'))
- final_averages: float32 [128, 16384], P('cls')
Inputs may be any that keep to these rules, and one draw needn't show every extreme that they name: `group_ids`: in every step, at most 6 of the 16 particles of one device name one class group; in every step some device's particles reach 6 for some group.
All inputs are finite; a program needn't handle non-finite values.
Results may differ from a plain program's by a relative error of at most 0.0027.
Values may be sent and summed in bfloat16 or wider, within the bound.
A program may use at most 256 MiB of HBM per device.

v0:
```python
import math

import jax
import jax.numpy as jnp
from jax import lax
from jax.sharding import PartitionSpec as P

RADII = 128
ANGLES = 128
ROT = 64
STEPS = 4
ASTEP = 2


def from_root(block, axis, owner):
    block = jnp.where(lax.axis_index(axis) == owner, block, jnp.zeros_like(block))
    return lax.psum(block, axis)


def rotate_each(images, shifts, angles):
    angle_idx = jnp.arange(angles, dtype=jnp.int32)
    index = (angle_idx[None, :] - shifts[:, None]) % angles
    return jnp.take_along_axis(images, index[:, None, :], axis=2)


def per_device(particles, averages, prior_mass, group_ids, class_ids, rot_ids, weights, owners):
    per_dev = particles.shape[0]
    pixels = particles.shape[1]
    groups = lax.axis_size("cls")
    per_group = averages.shape[0]
    capacity = per_dev * 3 // 8
    slots = groups * capacity
    cube = particles.reshape(per_dev, RADII, ANGLES)
    doubled = jnp.concatenate([cube, cube], axis=2)
    scale = 1.0 / math.sqrt(pixels)
    turns_block = min(ROT, max(8, 512 // per_dev))
    block_starts = list(range(0, ROT, turns_block))
    current = averages
    all_scores = []
    for step in range(STEPS):
        shifts = rot_ids[step] * ASTEP
        rotated = rotate_each(cube, shifts, ANGLES).reshape(per_dev, pixels)
        target = group_ids[step, :, 0]
        onehot_group = (target[:, None] == jnp.arange(groups, dtype=jnp.int32)[None, :]).astype(
            jnp.int32
        )
        rank = jnp.sum((jnp.cumsum(onehot_group, axis=0) - 1) * onehot_group, axis=1)
        slot_of = target * capacity + rank
        placing = (slot_of[None, :] == jnp.arange(slots, dtype=jnp.int32)[:, None]).astype(
            jnp.bfloat16
        )
        send_images = jnp.dot(placing, rotated, preferred_element_type=jnp.float32).astype(
            jnp.bfloat16
        )
        class_hot = (
            class_ids[step][:, None] == jnp.arange(per_group, dtype=jnp.int32)[None, :]
        ).astype(jnp.bfloat16)
        weighted_hot = class_hot * weights[step][:, None]
        send_weights = jnp.dot(placing, weighted_hot, preferred_element_type=jnp.float32).astype(
            jnp.bfloat16
        )
        got_images, got_weights = (
            lax.all_to_all(send_images, "cls", split_axis=0, concat_axis=0, tiled=True),
            lax.all_to_all(send_weights, "cls", split_axis=0, concat_axis=0, tiled=True),
        )
        partial_value = lax.dot_general(
            got_weights, got_images, (((0,), (0,)), ((), ())), preferred_element_type=jnp.float32
        )
        counts = jnp.sum(got_weights.astype(jnp.float32), axis=0)
        totals, mass = lax.psum((partial_value, counts), "dom")
        current = (prior_mass[:, None] * current + totals) / (prior_mass + mass)[:, None]
        refs = from_root(current.astype(jnp.bfloat16), "cls", owners[step])
        pieces = []
        for first in block_starts:
            count = min(turns_block, ROT - first)
            views = [
                doubled[:, :, ANGLES - turn * ASTEP : 2 * ANGLES - turn * ASTEP]
                for turn in range(first, first + count)
            ]
            rolled = jnp.stack(views, axis=1).reshape(per_dev * count, pixels)
            product = lax.dot_general(
                rolled, refs, (((1,), (1,)), ((), ())), preferred_element_type=jnp.float32
            )
            pieces.append(product.reshape(per_dev, count * per_group))
        stacked = jnp.concatenate(pieces, axis=1)
        all_scores.append(stacked * scale)
    return (jnp.stack(all_scores, axis=0), current)


def solution(mesh):
    return jax.shard_map(
        per_device,
        mesh=mesh,
        in_specs=(
            P(("dom", "cls"), None),
            P("cls", None),
            P("cls"),
            P(None, ("dom", "cls"), None),
            P(None, ("dom", "cls")),
            P(None, ("dom", "cls")),
            P(None, ("dom", "cls")),
            P(),
        ),
        out_specs=(P(None, ("dom", "cls"), None), P("cls", None)),
        check_vma=False,
    )
```

profile of v0, /device:TPU:0, one launch (start us, length us, event | category | flops | bytes accessed | tf_op | source)
XLA Modules:
  0.0 636.4 jit_solution(14930010265316669900)
XLA Ops:
  11.9 6.3 all-to-all-start.4
  20.6 11.1 %gather_fusion.2 = bf16[2048,128]{1,0:T(8,128)(2,1)S(1)} fusion(bf16[16,128,128]{1,2,0:T(8,128)(2,1)S(1)} %copy.11, s32[2048]{0:T(1024)S(1)} %get-tuple-element.116), kind=kCustom, calls=%fused_computation.2.clone | custom fusion | bytes 1064960 | tf_op jit(solution)/shard_map/jit(take_along_axis)/gather | solution.py:23
  32.9 5.1 all-to-all-start.2
  38.8 4.8 all-to-all-done.2
  43.6 3.2 all-to-all-start
  47.6 4.8 all-to-all-done
  52.4 3.2 all-to-all-start.6
  57.3 3.9 all-to-all-done.6
  61.2 3.5 all-to-all-start.5
  64.8 20.5 %gather_fusion.1 = bf16[2048,128]{1,0:T(8,128)(2,1)} fusion(bf16[16,128,128]{1,2,0:T(8,128)(2,1)S(1)} %copy.11, s32[2048]{0:T(1024)S(1)} %get-tuple-element.117), kind=kCustom, calls=%fused_computation.1.clone | custom fusion | bytes 1064960 | tf_op jit(solution)/shard_map/jit(take_along_axis)/gather | solution.py:23
  88.6 5.1 all-to-all-start.3
  93.6 20.5 %gather_fusion = bf16[2048,128]{1,0:T(8,128)(2,1)} fusion(bf16[16,128,128]{1,2,0:T(8,128)(2,1)S(1)} %copy.11, s32[2048]{0:T(1024)S(1)} %get-tuple-element.118), kind=kCustom, calls=%fused_computation.clone | custom fusion | bytes 1064960 | tf_op jit(solution)/shard_map/jit(take_along_axis)/gather | solution.py:23
  117.2 5.1 all-to-all-start.1
  122.3 11.1 %gather_fusion.3 = bf16[2048,128]{1,0:T(8,128)(2,1)S(1)} fusion(bf16[16,128,128]{1,2,0:T(8,128)(2,1)S(1)} %copy.11, s32[2048]{0:T(1024)S(1)} %get-tuple-element.115), kind=kCustom, calls=%fused_computation.3.clone | custom fusion | bytes 1064960 | tf_op jit(solution)/shard_map/jit(take_along_axis)/gather | solution.py:23
  135.7 7.3 %all-to-all-done.1 = bf16[4,6,16384]{2,1,0:T(8,128)(2,1)} async-done(((bf16[4,6,16384]{2,1,0:T(8,128)(2,1)}), bf16[4,6,16384]{2,1,0:T(8,128)(2,1)}, u32[]{:S(2)}, u32[]{:S(2)}) %all-to-all-start.1) | async-done | bytes 786464 | tf_op jit(solution)/shard_map/all_to_all | solution.py:63
  143.0 4.2 all-to-all-start.7
  151.5 1.9 convolution_bitcast_fusion.1
  153.4 3.2 convolution_bitcast_fusion.2
  156.6 3.1 convolution_bitcast_fusion.3
  159.7 9.9 %all-to-all-done.7 = bf16[4,6,16384]{2,1,0:T(8,128)(2,1)} async-done(((bf16[4,6,16384]{2,1,0:T(8,128)(2,1)}), bf16[4,6,16384]{2,1,0:T(8,128)(2,1)}, u32[]{:S(2)}, u32[]{:S(2)}) %all-to-all-start.7) | async-done | bytes 786464 | tf_op jit(solution)/shard_map/all_to_all | solution.py:63
  169.5 3.1 convolution_bitcast_fusion
  176.0 1.4 fusion.92
  178.7 1.4 fusion.90
  181.5 1.4 fusion.88
  182.9 1.4 fusion.87
  187.0 1.4 fusion.84
  192.6 1.4 fusion.80
  194.0 12.8 %all-reduce = (f32[32]{0:T(128)S(1)}, f32[32]{0:T(128)S(1)}, f32[32]{0:T(128)S(1)}, f32[32]{0:T(128)S(1)}) all-reduce(f32[32]{0:T(128)S(1)} %convert_reduce_fusion, f32[32]{0:T(128)S(1)} %convert_reduce_fusion.1, f32[32]{0:T(128)S(1)} %convert_reduce_fusion.2, f32[32]{0:T(128)S(1)} %convert_reduce_fusion.3), channel_id=1, replica_groups=mesh['dom'=8,'cls'=4] {'dom'}, use_global_device_ids=true, to_apply=%region_22.24 | all-reduce | flops 128 | bytes 1024 | tf_op jit(solution)/shard_map/psum | solution.py:70
  206.8 92.9 %all-reduce.6.cloned.1.call-done = (f32[32,16384]{1,0:T(8,128)}, f32[32,16384]{1,0:T(8,128)}, f32[32,16384]{1,0:T(8,128)}, f32[32,16384]{1,0:T(8,128)}) async-done(((f32[32,16384]{1,0:T(8,128)}, f32[32,16384]{1,0:T(8,128)}, f32[32,16384]{1,0:T(8,128)}, f32[32,16384]{1,0:T(8,128)}), (f32[32,16384]{1,0:T(8,128)}, f32[32,16384]{1,0:T(8,128)}, f32[32,16384]{1,0:T(8,128)}, ...) | async-done | bytes 8388624 | tf_op jit(solution)/shard_map/psum | solution.py:70
  299.7 4.2 convert_select_fusion.2
  303.9 4.9 convert_select_fusion
  308.9 1.4 fusion.79
  310.3 1.4 fusion.78
  319.9 1.4 fusion.71
  321.3 1.4 fusion.70
  324.0 1.4 fusion.68
  330.9 15.1 %copy.10 = bf16[16,32,128,128]{3,2,1,0:T(8,128)(2,1)} copy(bf16[16,32,128,128]{3,2,0,1:T(8,128)(2,1)} %get-tuple-element.21) | data formatting | bytes 33554432 | tf_op jit(solution)/shard_map/stack | solution.py:80
  346.0 1.9 copy-done
  348.0 6.7 %copy.14 = bf16[16,32,128,128]{3,2,1,0:T(8,128)(2,1)} copy(bf16[16,32,128,128]{3,2,0,1:T(8,128)(2,1)S(1)} %copy-done) | data formatting | bytes 33554432 | tf_op jit(solution)/shard_map/stack | solution.py:80
  354.6 110.6 %all-reduce.8.cloned.1.call-done = (bf16[32,16384]{1,0:T(8,128)(2,1)}, bf16[32,16384]{1,0:T(8,128)(2,1)}, bf16[32,16384]{1,0:T(8,128)(2,1)}, bf16[32,16384]{1,0:T(8,128)(2,1)}) async-done(((bf16[32,16384]{1,0:T(8,128)(2,1)}, bf16[32,16384]{1,0:T(8,128)(2,1)}, bf16[32,16384]{1,0:T(8,128)(2,1)}, bf16[32,16384]{1,0:T(8,128)(2,1)}), (bf16[32,16384]{1,0:T(8,128)(2,1)}, bf16[32,16384]{1,0:T(8,128)(2,1)}, ...) | async-done | bytes 4194320 | tf_op jit(solution)/shard_map/psum | solution.py:17
  465.2 23.1 %fusion.14 = f32[512,32]{1,0:T(8,128)S(1)} fusion(bf16[32,16384]{1,0:T(8,128)(2,1)} %get-tuple-element.14, bf16[64,8,128,128]{3,2,1,0:T(8,128)(2,1)} %bitcast.404), kind=kOutput, calls=%fused_computation.26 | convolution fusion | flops 536870912 | bytes 17891328 | tf_op jit(solution)/shard_map/dot_general | solution.py:81
  488.4 21.5 %fusion.6 = f32[512,32]{1,0:T(8,128)S(1)} fusion(bf16[32,16384]{1,0:T(8,128)(2,1)} %get-tuple-element.14, bf16[64,8,128,128]{3,2,1,0:T(8,128)(2,1)} %bitcast.410), kind=kOutput, calls=%fused_computation.18 | convolution fusion | flops 536870912 | bytes 17891328 | tf_op jit(solution)/shard_map/dot_general | solution.py:81
  509.9 17.4 %fusion.12 = f32[512,32]{1,0:T(8,128)S(1)} fusion(bf16[32,16384]{1,0:T(8,128)(2,1)S(1)} %copy-done.4, bf16[64,8,128,128]{3,2,1,0:T(8,128)(2,1)S(1)} %bitcast.407), kind=kOutput, calls=%fused_computation.24 | convolution fusion | flops 536870912 | bytes 17891328 | tf_op jit(solution)/shard_map/dot_general | solution.py:81
  527.3 21.0 %fusion.4 = f32[512,32]{1,0:T(8,128)S(1)} fusion(bf16[32,16384]{1,0:T(8,128)(2,1)} %get-tuple-element.13, bf16[64,8,128,128]{3,2,1,0:T(8,128)(2,1)} %bitcast.411), kind=kOutput, calls=%fused_computation.16 | convolution fusion | flops 536870912 | bytes 17891328 | tf_op jit(solution)/shard_map/dot_general | solution.py:81
  548.3 18.6 %fusion.10 = f32[512,32]{1,0:T(8,128)S(1)} fusion(bf16[32,16384]{1,0:T(8,128)(2,1)} %get-tuple-element.12, bf16[64,8,128,128]{3,2,1,0:T(8,128)(2,1)S(1)} %bitcast.408), kind=kOutput, calls=%fused_computation.22 | convolution fusion | flops 536870912 | bytes 17891328 | tf_op jit(solution)/shard_map/dot_general | solution.py:81
  566.9 21.0 %fusion.2 = f32[512,32]{1,0:T(8,128)S(1)} fusion(bf16[32,16384]{1,0:T(8,128)(2,1)} %get-tuple-element.12, bf16[64,8,128,128]{3,2,1,0:T(8,128)(2,1)} %bitcast.412), kind=kOutput, calls=%fused_computation.14 | convolution fusion | flops 536870912 | bytes 17891328 | tf_op jit(solution)/shard_map/dot_general | solution.py:81
  587.9 18.4 %fusion.8 = f32[512,32]{1,0:T(8,128)S(1)} fusion(bf16[32,16384]{1,0:T(8,128)(2,1)} %get-tuple-element.11, bf16[64,8,128,128]{3,2,1,0:T(8,128)(2,1)S(1)} %bitcast.409), kind=kOutput, calls=%fused_computation.20 | convolution fusion | flops 536870912 | bytes 17891328 | tf_op jit(solution)/shard_map/dot_general | solution.py:81
  606.3 20.8 %fusion = f32[512,32]{1,0:T(8,128)S(1)} fusion(bf16[32,16384]{1,0:T(8,128)(2,1)} %get-tuple-element.11, bf16[64,8,128,128]{3,2,1,0:T(8,128)(2,1)} %bitcast.413), kind=kOutput, calls=%fused_computation.12 | convolution fusion | flops 536870912 | bytes 17891328 | tf_op jit(solution)/shard_map/dot_general | solution.py:81
  (112 shorter events, 51.8 us)
Async XLA Ops:
  11.9 21.0 %all-to-all-start.4 = ((bf16[4,6,32]{2,1,0:T(8,128)(2,1)}), bf16[4,6,32]{2,1,0:T(8,128)(2,1)S(1)}, u32[]{:S(2)}, u32[]{:S(2)}) async-start(bf16[4,6,32]{2,1,0:T(8,128)(2,1)} %all_to_all.56), calls=%async_computation.4 | async-start | bytes 16384 | tf_op jit(solution)/shard_map/all_to_all | solution.py:64
  32.9 10.7 %all-to-all-start.2 = ((bf16[4,6,32]{2,1,0:T(8,128)(2,1)}), bf16[4,6,32]{2,1,0:T(8,128)(2,1)S(1)}, u32[]{:S(2)}, u32[]{:S(2)}) async-start(bf16[4,6,32]{2,1,0:T(8,128)(2,1)} %all_to_all.52), calls=%async_computation.2 | async-start | bytes 16384 | tf_op jit(solution)/shard_map/all_to_all | solution.py:64
  43.6 8.8 %all-to-all-start = ((bf16[4,6,32]{2,1,0:T(8,128)(2,1)}), bf16[4,6,32]{2,1,0:T(8,128)(2,1)S(1)}, u32[]{:S(2)}, u32[]{:S(2)}) async-start(bf16[4,6,32]{2,1,0:T(8,128)(2,1)} %all_to_all.48), calls=%async_computation | async-start | bytes 16384 | tf_op jit(solution)/shard_map/all_to_all | solution.py:64
  52.4 8.8 %all-to-all-start.6 = ((bf16[4,6,32]{2,1,0:T(8,128)(2,1)}), bf16[4,6,32]{2,1,0:T(8,128)(2,1)S(1)}, u32[]{:S(2)}, u32[]{:S(2)}) async-start(bf16[4,6,32]{2,1,0:T(8,128)(2,1)} %all_to_all.60), calls=%async_computation.6 | async-start | bytes 16384 | tf_op jit(solution)/shard_map/all_to_all | solution.py:64
  61.2 27.4 %all-to-all-start.5 = ((bf16[4,6,16384]{2,1,0:T(8,128)(2,1)}), bf16[4,6,16384]{2,1,0:T(8,128)(2,1)S(1)}, u32[]{:S(2)}, u32[]{:S(2)}) async-start(bf16[4,6,16384]{2,1,0:T(8,128)(2,1)} %all_to_all.58), calls=%async_computation.5 | async-start | bytes 2097152 | tf_op jit(solution)/shard_map/all_to_all | solution.py:63
  88.6 28.7 %all-to-all-start.3 = ((bf16[4,6,16384]{2,1,0:T(8,128)(2,1)}), bf16[4,6,16384]{2,1,0:T(8,128)(2,1)}, u32[]{:S(2)}, u32[]{:S(2)}) async-start(bf16[4,6,16384]{2,1,0:T(8,128)(2,1)} %all_to_all.54), calls=%async_computation.3 | async-start | bytes 2097152 | tf_op jit(solution)/shard_map/all_to_all | solution.py:63
  117.2 25.8 %all-to-all-start.1 = ((bf16[4,6,16384]{2,1,0:T(8,128)(2,1)}), bf16[4,6,16384]{2,1,0:T(8,128)(2,1)}, u32[]{:S(2)}, u32[]{:S(2)}) async-start(bf16[4,6,16384]{2,1,0:T(8,128)(2,1)} %all_to_all.50), calls=%async_computation.1 | async-start | bytes 2097152 | tf_op jit(solution)/shard_map/all_to_all | solution.py:63
  134.2 38.5 %copy-start.2 = (s32[4]{0:T(128)S(1)}, s32[4]{0:T(128)}, u32[]{:S(2)}) copy-start(s32[4]{0:T(128)} %param.17) | copy-start | bytes 52
  143.0 26.5 %all-to-all-start.7 = ((bf16[4,6,16384]{2,1,0:T(8,128)(2,1)}), bf16[4,6,16384]{2,1,0:T(8,128)(2,1)}, u32[]{:S(2)}, u32[]{:S(2)}) async-start(bf16[4,6,16384]{2,1,0:T(8,128)(2,1)} %all_to_all.62), calls=%async_computation.7 | async-start | bytes 2097152 | tf_op jit(solution)/shard_map/all_to_all | solution.py:63
  147.3 152.4 %all-reduce.6.cloned.1.call-start = ((), (), s32[]{:S(2)}) async-start(), calls=%async_computation.8 | async-start | bytes 16777216 | tf_op jit(solution)/shard_map/psum | solution.py:70
  172.6 34.2 %copy-start.3 = (f32[32]{0:T(128)S(1)}, f32[32]{0:T(128)}, u32[]{:S(2)}) copy-start(f32[32]{0:T(128)} %param.12) | copy-start | bytes 388
  172.6 127.0 %copy-start.1 = (f32[32,16384]{1,0:T(8,128)S(1)}, f32[32,16384]{1,0:T(8,128)}, u32[]{:S(2)}) copy-start(f32[32,16384]{1,0:T(8,128)} %param.11) | copy-start | bytes 6291460
  172.7 292.6 %all-reduce.8.cloned.1.call-start = ((), (), s32[]{:S(2)}) async-start(), calls=%async_computation.9 | async-start | bytes 8388608 | tf_op jit(solution)/shard_map/psum | solution.py:17
  330.9 17.1 %copy-start = (bf16[16,32,128,128]{3,2,0,1:T(8,128)(2,1)S(1)}, bf16[16,32,128,128]{3,2,0,1:T(8,128)(2,1)}, u32[]{:S(2)}) copy-start(bf16[16,32,128,128]{3,2,0,1:T(8,128)(2,1)} %get-tuple-element.22) | copy-start | bytes 50331652
  465.2 44.6 %slice-start = ((s8[16777216]{0:T(1024)(128)(4,1)}), s8[4194304]{0:T(1024)(128)(4,1)S(1)}, s32[]{:S(2)}) async-start(s8[16777216]{0:T(1024)(128)(4,1)} %bitcast.405), calls=%async_computation.10 | async-start | bytes 8388608
  465.2 44.6 %slice-start.1 = ((s8[16777216]{0:T(1024)(128)(4,1)}), s8[4194304]{0:T(1024)(128)(4,1)S(1)}, s32[]{:S(2)}) async-start(s8[16777216]{0:T(1024)(128)(4,1)} %bitcast.405), calls=%async_computation.11 | async-start | bytes 8388608
  488.3 21.6 %copy-start.4 = (bf16[32,16384]{1,0:T(8,128)(2,1)S(1)}, bf16[32,16384]{1,0:T(8,128)(2,1)}, u32[]{:S(2)}) copy-start(bf16[32,16384]{1,0:T(8,128)(2,1)} %get-tuple-element.13) | copy-start | bytes 3145732
  488.3 21.6 %slice-start.2 = ((s8[16777216]{0:T(1024)(128)(4,1)}), s8[4194304]{0:T(1024)(128)(4,1)S(1)}, s32[]{:S(2)}) async-start(s8[16777216]{0:T(1024)(128)(4,1)} %bitcast.405), calls=%async_computation.12 | async-start | bytes 8388608
  488.4 21.6 %slice-start.3 = ((s8[16777216]{0:T(1024)(128)(4,1)}), s8[4194304]{0:T(1024)(128)(4,1)S(1)}, s32[]{:S(2)}) async-start(s8[16777216]{0:T(1024)(128)(4,1)} %bitcast.405), calls=%async_computation.13 | async-start | bytes 8388608
Sparse Core Ops, SparseCore 0:
  172.8 126.8 all-reduce.5
  309.0 156.1 all-reduce.7
where the time goes:
time: 644 us; the launch traced here: 636 us
  waiting for transfers between devices  234 us (36%)
  matrix products  175 us (27%)
  local copies, waits for them, and re-layouts  148 us (23%)
  starting transfers between devices  36.1 us (6%)
  between operations  17.4 us (3%)
  other arithmetic  13 us (2%)
  blocking collectives  12.8 us (2%)
    dot_general x8, matrix products, per_device(): lax.dot_general(rolled, refs, (((1,), (1,)), ((), ())), preferred_element...  162 us
    psum x1, waiting for transfers between devices, from_root(): return lax.psum(block, axis)  111 us
    psum x1, waiting for transfers between devices, per_device(): totals, mass = lax.psum((partial_value, counts), 'dom')  92.9 us
    gather x8, local copies, waits for them, and re-layouts, rotate_each(): return jnp.take_along_axis(images, index[:, None, :], axis=2)  66.5 us
    unnamed x51, local copies, waits for them, and re-layouts  45.8 us
    another operation x3, local copies, waits for them, and re-layouts, per_device(): rolled = jnp.stack(views, axis=1).reshape(per_dev * count, pixels)  23.2 us
    all_to_all x4, starting transfers between devices, per_device(): lax.all_to_all(send_images, 'cls', split_axis=0, concat_axis=0, tiled=True)  17.9 us
    all_to_all x4, starting transfers between devices, per_device(): lax.all_to_all(send_weights, 'cls', split_axis=0, concat_axis=0, tiled=True)  17.9 us
  transfers between devices with their start and end apart: 10, of which 7 were waited for; matrix products, arithmetic and copies ran while one was open for 23% of the time, Pallas kernels for 0%

commit v1 on v0

v1 whole, which is shorter than its diff:
```python
import functools
import math

import jax
import jax.numpy as jnp
from jax import lax
from jax.experimental import pallas as pl
from jax.experimental.pallas import tpu as pltpu
from jax.sharding import PartitionSpec as P

RADII = 128
ANGLES = 128
ROT = 64
STEPS = 4
ASTEP = 2
MIB = 1024 * 1024


def update_kernel(owners_ref, parts_ref, av_ref, label_ref, weight_ref, shift_ref, prior_ref, refs_ref, final_ref):
    count, width = parts_ref.shape
    classes = av_ref.shape[0]
    per_group = refs_ref.shape[0] // STEPS
    radii = width // ANGLES
    prior = prior_ref[...]
    lane = lax.broadcasted_iota(jnp.int32, (count, ANGLES), 1)
    class_row = lax.broadcasted_iota(jnp.int32, (classes, count), 0)
    final_ref[...] = av_ref[...]
    for step in range(STEPS):
        index = (lane - shift_ref[:, step : step + 1]) & (ANGLES - 1)
        hot = jnp.where(class_row == label_ref[step : step + 1, :], weight_ref[step : step + 1, :], 0.0)
        mass = jnp.sum(hot, axis=1, keepdims=True)
        hot = hot.astype(jnp.bfloat16)
        inverse = 1.0 / (prior + mass)
        for a in range(radii):
            cols = slice(a * ANGLES, (a + 1) * ANGLES)
            image = parts_ref[:, cols].astype(jnp.float32)
            turned = jnp.take_along_axis(image, index, axis=1).astype(jnp.bfloat16)
            totals = jnp.dot(hot, turned, preferred_element_type=jnp.float32)
            final_ref[:, cols] = (prior * final_ref[:, cols] + totals) * inverse
        start = pl.multiple_of(owners_ref[step] * per_group, per_group)
        refs_ref[step * per_group : (step + 1) * per_group, :] = final_ref[pl.ds(start, per_group), :].astype(
            jnp.bfloat16
        )


def score_kernel(parts_ref, refs_ref, out_ref, rolled, total):
    step = pl.program_id(0)
    per_dev = parts_ref.shape[0]
    blocks, names, width = refs_ref.shape
    per_group = names // STEPS
    radii = parts_ref.shape[1] // ANGLES
    for a in range(radii):
        cols = slice(a * ANGLES, (a + 1) * ANGLES)
        image = parts_ref[:, cols]
        for r in range(ROT):
            turned = pltpu.roll(image, r * ASTEP, 1) if r else image
            rolled[r * per_dev : (r + 1) * per_dev, cols] = turned
    product = None
    for b in range(blocks):
        part = lax.dot_general(
            rolled[:, b * width : (b + 1) * width],
            refs_ref[b],
            (((1,), (1,)), ((), ())),
            preferred_element_type=jnp.float32,
        )
        product = part if product is None else product + part

    @pl.when(step == 0)
    def _():
        total[...] = product

    @pl.when(step > 0)
    def _():
        total[...] += product

    @pl.when(step == pl.num_programs(0) - 1)
    def _():
        scale = 1.0 / math.sqrt(RADII * ANGLES)
        pack = 128 // per_group
        for q in range(ROT // pack):
            tiles = [total[(q * pack + j) * per_dev : (q * pack + j + 1) * per_dev, :] * scale for j in range(pack)]
            for s in range(STEPS):
                out_ref[s, :, q * 128 : (q + 1) * 128] = jnp.concatenate(
                    [t[:, s * per_group : (s + 1) * per_group] for t in tiles], axis=1
                )


def per_device(particles, averages, prior_mass, group_ids, class_ids, rot_ids, weights, owners):
    per_dev, pixels = particles.shape
    per_group = averages.shape[0]
    doms, groups = lax.axis_size("dom"), lax.axis_size("cls")
    devices = doms * groups
    width = pixels // devices
    count = per_dev * devices
    classes = per_group * groups
    everywhere = ("dom", "cls")

    label = (group_ids[:, :, 0] * per_group + class_ids).astype(jnp.float32)
    shift = (rot_ids * ASTEP).astype(jnp.float32)
    meta = jnp.stack([label, shift, weights.astype(jnp.float32)])
    flat = jnp.concatenate([meta.reshape(-1), prior_mass])
    gathered = lax.all_gather(flat, everywhere, axis=0, tiled=False)
    size = 3 * STEPS * per_dev
    meta = gathered[:, :size].reshape(devices, 3, STEPS, per_dev).transpose(1, 2, 0, 3).reshape(3, STEPS, count)
    prior = gathered[:groups, size:].reshape(classes, 1)

    mine = lax.all_to_all(
        particles.reshape(per_dev, devices, width).transpose(1, 0, 2), everywhere, split_axis=0, concat_axis=0, tiled=True
    ).reshape(count, width)
    band = lax.dynamic_slice_in_dim(averages, lax.axis_index("dom") * groups * width, groups * width, 1)
    band = lax.all_to_all(
        band.reshape(per_group, groups, width).transpose(1, 0, 2), "cls", split_axis=0, concat_axis=0, tiled=True
    ).reshape(classes, width)

    vmem = pl.BlockSpec(memory_space=pltpu.VMEM)
    refs, final = pl.pallas_call(
        update_kernel,
        out_shape=(
            jax.ShapeDtypeStruct((STEPS * per_group, width), jnp.bfloat16),
            jax.ShapeDtypeStruct((classes, width), jnp.float32),
        ),
        in_specs=[pl.BlockSpec(memory_space=pltpu.SMEM)] + [vmem] * 6,
        out_specs=(vmem, vmem),
        compiler_params=pltpu.CompilerParams(vmem_limit_bytes=40 * MIB),
        name="update",
    )(owners, mine, band, meta[0].astype(jnp.int32), meta[2], meta[1].astype(jnp.int32).T, prior)

    all_refs = lax.all_gather(refs, everywhere, axis=0, tiled=False)
    last = lax.all_to_all(
        final.astype(jnp.bfloat16).reshape(groups, per_group, width), "cls", split_axis=0, concat_axis=0, tiled=True
    )
    last = lax.all_gather(last, "dom", axis=0, tiled=False)
    last = last.transpose(2, 0, 1, 3).reshape(per_group, pixels).astype(jnp.float32)

    chunks = 8
    scores = pl.pallas_call(
        score_kernel,
        grid=(chunks,),
        out_shape=jax.ShapeDtypeStruct((STEPS, per_dev, ROT * per_group), jnp.float32),
        in_specs=[
            pl.BlockSpec((per_dev, pixels // chunks), lambda c: (0, c)),
            pl.BlockSpec((devices // chunks, STEPS * per_group, width), lambda c: (c, 0, 0)),
        ],
        out_specs=pl.BlockSpec((STEPS, per_dev, ROT * per_group), lambda c: (0, 0, 0)),
        scratch_shapes=[
            pltpu.VMEM((ROT * per_dev, pixels // chunks), jnp.bfloat16),
            pltpu.VMEM((ROT * per_dev, STEPS * per_group), jnp.float32),
        ],
        compiler_params=pltpu.CompilerParams(vmem_limit_bytes=40 * MIB),
        name="scores",
    )(particles, all_refs)
    return scores, last


def solution(mesh):
    return jax.shard_map(
        per_device,
        mesh=mesh,
        in_specs=(
            P(("dom", "cls"), None),
            P("cls", None),
            P("cls"),
            P(None, ("dom", "cls"), None),
            P(None, ("dom", "cls")),
            P(None, ("dom", "cls")),
            P(None, ("dom", "cls")),
            P(),
        ),
        out_specs=(P(None, ("dom", "cls"), None), P("cls", None)),
        check_vma=False,
    )
```

time: 644 us -> 205 us (0.32); the launches traced: 636 us -> 204 us
  matrix products: 175 us -> 0 us
  waiting for transfers between devices: 234 us -> 88.4 us
  local copies, waits for them, and re-layouts: 148 us -> 19.6 us
  blocking collectives: 12.8 us -> 50.6 us
  starting transfers between devices: 36.1 us -> 10.1 us
  Pallas kernels: 0 us -> 18.3 us
  other arithmetic: 13 us -> 3.15 us
    psum x2 -> x0, waiting for transfers between devices: 203 us -> none  [the longest x1 111 us: from_root(): return lax.psum(block, axis)]
    dot_general x20 -> x0, matrix products: 175 us -> none  [the longest x8 162 us: per_device(): lax.dot_general(rolled, refs, (((1,), (1,)), ((), ())), preferred_element...]
    all_gather x0 -> x2, waiting for transfers between devices: none -> 79.6 us  [the longest x1 57.8 us: per_device(): all_refs = lax.all_gather(refs, everywhere, axis=0, tiled=False)]
    gather x8 -> x0, local copies, waits for them, and re-layouts: 66.5 us -> none  [rotate_each(): return jnp.take_along_axis(images, index[:, None, :], axis=2)]
    unnamed x0 -> x1, blocking collectives: none -> 40.9 us
    unnamed x51 -> x23, local copies, waits for them, and re-layouts: 45.8 us -> 5.36 us
    all_to_all x8 -> x2, starting transfers between devices: 35.8 us -> 9.98 us  [the longest x1 6.32 us: per_device(): lax.all_to_all(band.reshape(per_group, groups, width).transpose(1, 0, 2),...]
    another operation x3 -> x0, local copies, waits for them, and re-layouts: 23.2 us -> none  [per_device(): rolled = jnp.stack(views, axis=1).reshape(per_dev * count, pixels)]
  transfers between devices with their start and end apart: 10 -> 4, of which waited for: 7 -> 3; matrix products, arithmetic and copies ran while one was open for 23% -> 8% of each run, Pallas kernels for 0% -> 0%
where the time goes in v1:
time: 205 us; the launch traced here: 204 us
  waiting for transfers between devices  88.4 us (43%)
  blocking collectives  50.6 us (25%)
  local copies, waits for them, and re-layouts  19.6 us (10%)
  Pallas kernels  18.3 us (9%)
  between operations  14.2 us (7%)
  starting transfers between devices  10.1 us (5%)
  other arithmetic  3.15 us (2%)
    all_gather x1, waiting for transfers between devices, per_device(): all_refs = lax.all_gather(refs, everywhere, axis=0, tiled=False)  57.8 us
    unnamed x1, blocking collectives  40.9 us
    all_gather x1, waiting for transfers between devices, per_device(): last = lax.all_gather(last, 'dom', axis=0, tiled=False)  21.8 us
    pallas_call x1, Pallas kernels, per_device(): pl.pallas_call(score_kernel, grid=(chunks,), out_shape=jax.ShapeDtypeStru...  15.3 us
    all_to_all x1, blocking collectives, per_device(): lax.all_to_all(final.astype(jnp.bfloat16).reshape(groups, per_group, widt...  9.63 us
    all_to_all x1, waiting for transfers between devices, per_device(): lax.all_to_all(band.reshape(per_group, groups, width).transpose(1, 0, 2),...  8.05 us
    convert_element_type x2, local copies, waits for them, and re-layouts, per_device(): last.transpose(2, 0, 1, 3).reshape(per_group, pixels).astype(jnp.float32)  6.36 us
    all_to_all x1, starting transfers between devices, per_device(): lax.all_to_all(band.reshape(per_group, groups, width).transpose(1, 0, 2),...  6.32 us
  transfers between devices with their start and end apart: 4, of which 3 were waited for; matrix products, arithmetic and copies ran while one was open for 8% of the time, Pallas kernels for 0%

profile of v1, /device:TPU:0, one launch (start us, length us, event | category | flops | bytes accessed | tf_op | source)
XLA Modules:
  0.0 204.3 jit_solution(8087687448867202377)
XLA Ops:
  7.2 0.0 copy-start
  7.2 0.0 copy-start.2
  7.2 1.6 copy-done
  8.8 0.0 copy-start.10
  8.8 0.2 reshape.44
  9.0 0.0 copy-start.5
  9.0 0.8 copy.33
  9.8 6.3 %all-to-all-start.1 = ((f32[4,32,512]{2,1,0:T(8,128)}), f32[4,32,512]{2,1,0:T(8,128)S(1)}, u32[]{:S(2)}, u32[]{:S(2)}) async-start(f32[4,32,512]{2,1,0:T(8,128)} %copy.33), calls=%async_computation.1 | async-start | bytes 524288 | tf_op jit(solution)/shard_map/all_to_all | solution.py:111
  16.1 0.0 copy-done.2
  16.1 0.9 copy.42
  17.0 8.0 %all-to-all-done.1 = f32[4,32,512]{2,1,0:T(8,128)S(1)} async-done(((f32[4,32,512]{2,1,0:T(8,128)}), f32[4,32,512]{2,1,0:T(8,128)S(1)}, u32[]{:S(2)}, u32[]{:S(2)}) %all-to-all-start.1) | async-done | bytes 262176 | tf_op jit(solution)/shard_map/all_to_all | solution.py:111
  25.0 3.7 %all-to-all-start = ((bf16[32,16,512]{2,1,0:T(8,128)(2,1)}), bf16[32,16,512]{2,1,0:T(8,128)(2,1)S(1)}, u32[]{:S(2)}, u32[]{:S(2)}) async-start(bf16[32,16,512]{2,1,0:T(8,128)(2,1)} %bitcast.40), calls=%async_computation | async-start | bytes 1048576 | tf_op jit(solution)/shard_map/all_to_all | solution.py:107
  28.7 0.0 all-gather.8.cloned.1.call-start
  28.8 0.0 copy-done.9
  28.8 0.0 copy-done.8
  28.8 0.0 copy-done.6
  28.8 0.0 copy-done.7
  28.8 0.1 reshape.46
  28.9 0.0 copy-done.10
  28.9 0.2 maximum_dynamic-update-slice_fusion
  29.1 40.9 %all-reduce = f32[7168]{0:T(1024)S(1)} all-reduce(f32[7168]{0:T(1024)S(1)} %maximum_dynamic-update-slice_fusion), channel_id=2, replica_groups=mesh['dom'=8,'cls'=4] {'dom','cls'}, use_global_device_ids=true, to_apply=%add | all-reduce | flops 7168 | bytes 57344
  70.1 0.1 reshape.52
  70.1 0.1 slice.27
  70.2 0.1 reshape.58.prior_ref
  70.3 0.7 copy.34
  71.1 1.4 slice_convert_fusion
  72.5 0.8 copy.36
  73.3 0.1 squeeze.2.weight_ref
  73.4 1.5 copy.35
  74.9 0.9 convert_element_type.33.label_ref
  75.8 1.6 copy.37
  77.5 0.0 all-to-all-done
  77.5 0.0 copy-done.5
  77.5 0.9 copy-done.3
  78.4 3.0 %update.1 = (bf16[128,512]{1,0:T(8,128)(2,1)S(1)}, f32[128,512]{1,0:T(8,128)S(1)}) custom-call(s32[4]{0:T(128)S(1)} %copy-done.5, bf16[512,512]{1,0:T(8,128)(2,1)S(1)} %bitcast.37, f32[128,512]{1,0:T(8,128)S(1)} %bitcast.38, s32[4,512]{1,0:T(4,128)S(1)} %convert_element_type.33.label_ref, f32[4,512]{1,0:T(4,128)S(1)} %squeeze.2.weight_ref, ...), custom_call_target="tpu_custom_call" | custom-call | tf_op jit(solution)/shard_map/update/pallas_call | solution.py:116
  81.4 0.0 copy-start.4
  81.4 0.6 copy-done.4
  82.1 9.6 %all_to_all.15 = bf16[4,32,512]{2,1,0:T(8,128)(2,1)} all-to-all(bf16[4,32,512]{2,1,0:T(8,128)(2,1)S(1)} %bitcast.43), channel_id=1, replica_groups=mesh['dom'=8,'cls'=4] {'cls'}, dimensions={0} | all-to-all | bytes 262144 | tf_op jit(solution)/shard_map/all_to_all | solution.py:129
  91.7 0.0 all-gather.8.cloned.1.call-update
  91.7 0.0 all-gather.6.cloned.1.call-start
  91.8 0.7 all-gather.6.cloned.1.call-update
  92.5 21.8 %all-gather.8.cloned.1.call-done = bf16[32,32,512]{2,1,0:T(8,128)(2,1)} async-done(((bf16[4,32,512]{2,1,0:T(8,128)(2,1)}), bf16[32,32,512]{2,1,0:T(8,128)(2,1)}) %all-gather.8.cloned.1.call-update) | async-done | bytes 1048592 | tf_op jit(solution)/shard_map/all_gather | solution.py:132
  114.3 1.5 convert_bitcast_fusion
  115.8 2.7 %copy.39 = f32[32,8,4,512]{3,2,1,0:T(4,128)} copy(f32[32,8,4,512]{3,0,2,1:T(8,128)S(1)} %convert_bitcast_fusion) | data formatting | bytes 4194304 | tf_op jit(solution)/shard_map/convert_element_type | solution.py:133
  118.5 3.7 %reshape.51 = f32[32,16384]{1,0:T(8,128)} reshape(f32[32,8,4,512]{3,2,1,0:T(4,128)} %copy.39) | data formatting | bytes 4194304 | tf_op jit(solution)/shard_map/convert_element_type | solution.py:133
  122.1 57.8 %all-gather.6.cloned.1.call-done = bf16[4096,512]{1,0:T(8,128)(2,1)} async-done(((bf16[128,512]{1,0:T(8,128)(2,1)}), bf16[4096,512]{1,0:T(8,128)(2,1)}) %all-gather.6.cloned.1.call-update) | async-done | bytes 4194320 | tf_op jit(solution)/shard_map/all_gather | solution.py:128
  180.0 2.2 %copy-done.1 = bf16[4096,512]{1,0:T(8,128)(2,1)S(1)} copy-done((bf16[4096,512]{1,0:T(8,128)(2,1)S(1)}, bf16[4096,512]{1,0:T(8,128)(2,1)}, u32[]{:S(2)}) %copy-start.1) | copy-done | bytes 4194328
  182.1 15.3 %scores.1 = f32[4,16,2048]{2,1,0:T(8,128)} custom-call(bf16[16,16384]{1,0:T(8,128)(2,1)S(1)} %copy-done.2, bf16[32,128,512]{2,1,0:T(8,128)(2,1)S(1)} %bitcast.35), custom_call_target="tpu_custom_call" | custom-call | tf_op jit(solution)/shard_map/scores/pallas_call | solution.py:136
  (13 shorter events, 0.1 us)
Async XLA Ops:
  7.2 1.6 copy-start
  7.2 8.9 %copy-start.2 = (bf16[16,16384]{1,0:T(8,128)(2,1)S(1)}, bf16[16,16384]{1,0:T(8,128)(2,1)}, u32[]{:S(2)}) copy-start(bf16[16,16384]{1,0:T(8,128)(2,1)} %parts_ref.1) | copy-start | bytes 1572868
  8.8 20.0 %copy-start.9 = (bf16[4,16]{1,0:T(4,128)(2,1)S(1)}, bf16[4,16]{1,0:T(4,128)(2,1)}, u32[]{:S(2)}) copy-start(bf16[4,16]{1,0:T(4,128)(2,1)} %param.14) | copy-start | bytes 388
  8.8 20.0 %copy-start.8 = (s32[4,16,1]{1,2,0:T(1,128)S(1)}, s32[4,16,1]{1,2,0:T(1,128)}, u32[]{:S(2)}) copy-start(s32[4,16,1]{1,2,0:T(1,128)} %param.11) | copy-start | bytes 772
  8.8 20.0 %copy-start.6 = (s32[4,16]{1,0:T(4,128)S(1)}, s32[4,16]{1,0:T(4,128)}, u32[]{:S(2)}) copy-start(s32[4,16]{1,0:T(4,128)} %param.13) | copy-start | bytes 772
  8.8 20.0 %copy-start.7 = (s32[4,16]{1,0:T(4,128)S(1)}, s32[4,16]{1,0:T(4,128)}, u32[]{:S(2)}) copy-start(s32[4,16]{1,0:T(4,128)} %param.12) | copy-start | bytes 772
  8.8 20.2 %copy-start.10 = (f32[32]{0:T(128)S(1)}, f32[32]{0:T(128)}, u32[]{:S(2)}) copy-start(f32[32]{0:T(128)} %param.10) | copy-start | bytes 388
  9.0 68.5 %copy-start.5 = (s32[4]{0:T(128)S(1)}, s32[4]{0:T(128)}, u32[]{:S(2)}) copy-start(s32[4]{0:T(128)} %owners_ref.1) | copy-start | bytes 52
  9.8 15.2 %all-to-all-start.1 = ((f32[4,32,512]{2,1,0:T(8,128)}), f32[4,32,512]{2,1,0:T(8,128)S(1)}, u32[]{:S(2)}, u32[]{:S(2)}) async-start(f32[4,32,512]{2,1,0:T(8,128)} %copy.33), calls=%async_computation.1 | async-start | bytes 524288 | tf_op jit(solution)/shard_map/all_to_all | solution.py:111
  25.0 52.5 %all-to-all-start = ((bf16[32,16,512]{2,1,0:T(8,128)(2,1)}), bf16[32,16,512]{2,1,0:T(8,128)(2,1)S(1)}, u32[]{:S(2)}, u32[]{:S(2)}) async-start(bf16[32,16,512]{2,1,0:T(8,128)(2,1)} %bitcast.40), calls=%async_computation | async-start | bytes 1048576 | tf_op jit(solution)/shard_map/all_to_all | solution.py:107
  28.7 85.6 %all-gather.8.cloned.1.call-start = ((), (), s32[]{:S(2)}) async-start(), calls=%async_computation.4 | async-start | bytes 1179648 | tf_op jit(solution)/shard_map/all_gather | solution.py:132
  77.5 1.0 copy-start.3
  81.4 0.7 copy-start.4
  91.7 88.2 %all-gather.6.cloned.1.call-start = ((), (), s32[]{:S(2)}) async-start(), calls=%async_computation.3 | async-start | bytes 4325376 | tf_op jit(solution)/shard_map/all_gather | solution.py:128
  179.9 2.2 %copy-start.1 = (bf16[4096,512]{1,0:T(8,128)(2,1)S(1)}, bf16[4096,512]{1,0:T(8,128)(2,1)}, u32[]{:S(2)}) copy-start(bf16[4096,512]{1,0:T(8,128)(2,1)} %all-gather.6.cloned.1.call-done) | copy-start | bytes 12582916
Sparse Core Ops, SparseCore 0:
  91.8 22.3 all-gather.7
  117.8 62.0 all-gather.5

commit v2 on v1

--- a/solution.py
+++ b/solution.py
@@ -16,15 +16,17 @@
 MIB = 1024 * 1024
 
 
-def update_kernel(owners_ref, parts_ref, av_ref, label_ref, weight_ref, shift_ref, prior_ref, refs_ref, final_ref):
-    count, width = parts_ref.shape
-    classes = av_ref.shape[0]
-    per_group = refs_ref.shape[0] // STEPS
+def update_kernel(owners_ref, parts_ref, av_ref, label_ref, weight_ref, shift_ref, prior_ref, refs_ref, last_ref, current):
+    senders, rows = parts_ref.shape[:2]
+    groups, padded, width = av_ref.shape
+    per_group = last_ref.shape[1]
     radii = width // ANGLES
+    per_dev = rows // (radii + 1)
+    count, classes = senders * per_dev, groups * per_group
     prior = prior_ref[...]
     lane = lax.broadcasted_iota(jnp.int32, (count, ANGLES), 1)
     class_row = lax.broadcasted_iota(jnp.int32, (classes, count), 0)
-    final_ref[...] = av_ref[...]
+    current[...] = av_ref[:, :per_group, :].reshape(classes, width)
     for step in range(STEPS):
         index = (lane - shift_ref[:, step : step + 1]) & (ANGLES - 1)
         hot = jnp.where(class_row == label_ref[step : step + 1, :], weight_ref[step : step + 1, :], 0.0)
@@ -33,14 +35,105 @@
         inverse = 1.0 / (prior + mass)
         for a in range(radii):
             cols = slice(a * ANGLES, (a + 1) * ANGLES)
-            image = parts_ref[:, cols].astype(jnp.float32)
+            image = parts_ref[:, a * per_dev : (a + 1) * per_dev, :].reshape(count, ANGLES).astype(jnp.float32)
             turned = jnp.take_along_axis(image, index, axis=1).astype(jnp.bfloat16)
             totals = jnp.dot(hot, turned, preferred_element_type=jnp.float32)
-            final_ref[:, cols] = (prior * final_ref[:, cols] + totals) * inverse
+            current[:, cols] = (prior * current[:, cols] + totals) * inverse
         start = pl.multiple_of(owners_ref[step] * per_group, per_group)
-        refs_ref[step * per_group : (step + 1) * per_group, :] = final_ref[pl.ds(start, per_group), :].astype(
-            jnp.bfloat16
+        refs_ref[step * per_group : (step + 1) * per_group, :] = current[pl.ds(start, per_group), :].astype(jnp.bfloat16)
+    last_ref[...] = current[...].astype(jnp.bfloat16).reshape(groups, per_group, width)
+
+
+def gather_kernel(doms, groups, refs_ref, final_ref, slots_ref, last_ref, own_sem, z_send, z_recv, d_send, d_recv):
+    dom, cls = lax.axis_index("dom"), lax.axis_index("cls")
+    bits = doms.bit_length() - 1
+    per_group, width = final_ref.shape[1:]
+
+    def across(bit):
+        return dom + (1 << bit) - (2 << bit) * (lax.div(dom, 1 << bit) % 2)
+
+    def peer(hop):
+        return lax.rem(cls + hop, groups)
+
+    barrier = pltpu.get_barrier_semaphore()
+    for hop in range(1, groups):
+        pl.semaphore_signal(barrier, device_id={"dom": dom, "cls": peer(hop)}, device_id_type=pl.DeviceIdType.MESH)
+    for bit in range(bits):
+        pl.semaphore_signal(barrier, device_id={"dom": across(bit), "cls": cls}, device_id_type=pl.DeviceIdType.MESH)
+    pl.semaphore_wait(barrier, groups - 1 + bits)
+
+    def columns(which_dom, which_cls, count):
+        return pl.ds(pl.multiple_of((which_dom * groups + which_cls) * width, width), count * width)
+
+    own = [
+        pltpu.make_async_copy(refs_ref, slots_ref.at[dom, cls], own_sem.at[0]),
+        pltpu.make_async_copy(final_ref.at[cls], last_ref.at[:, columns(dom, cls, 1)], own_sem.at[1]),
+    ]
+    sent = []
+    for hop in range(1, groups):
+        target = {"dom": dom, "cls": peer(hop)}
+        moves = [
+            pltpu.make_async_remote_copy(
+                refs_ref, slots_ref.at[dom, cls], z_send.at[0, hop], z_recv.at[0, hop], target, pl.DeviceIdType.MESH
+            ),
+            pltpu.make_async_remote_copy(
+                final_ref.at[peer(hop)],
+                last_ref.at[:, columns(dom, cls, 1)],
+                z_send.at[1, hop],
+                z_recv.at[1, hop],
+                target,
+                pl.DeviceIdType.MESH,
+            ),
+        ]
+        for move in moves:
+            move.start()
+        sent.extend(moves)
+    for copy in own:
+        copy.start()
+    for copy in own:
+        copy.wait()
+    for move in sent:
+        move.wait_recv()
+
+    def part(half, which_dom):
+        span = groups // 2
+        rows = per_group // 2
+        return (
+            slots_ref.at[which_dom, half * span : (half + 1) * span],
+            last_ref.at[half * rows : (half + 1) * rows, columns(which_dom, 0, groups)],
         )
+
+    orders = [list(range(1, bits)) + [0], list(range(bits - 1, 0, -1)) + [0]]
+    for stage in range(bits):
+        moves = []
+        for half, order in enumerate(orders):
+            bit = order[stage]
+            done = order[:stage]
+            target = {"dom": across(bit), "cls": cls}
+            for pick in range(1 << stage):
+                slot = dom
+                for place, old in enumerate(done):
+                    if pick >> place & 1:
+                        slot = slot + (1 << old) - (2 << old) * (lax.div(dom, 1 << old) % 2)
+                for kind, piece in enumerate(part(half, slot)):
+                    spot = (1 << stage) - 1 + pick
+                    moves.append(
+                        pltpu.make_async_remote_copy(
+                            piece,
+                            piece,
+                            d_send.at[half, kind, spot],
+                            d_recv.at[half, kind, spot],
+                            target,
+                            pl.DeviceIdType.MESH,
+                        )
+                    )
+        for move in moves:
+            move.start()
+        for move in moves:
+            move.wait_recv()
+        sent.extend(moves)
+    for move in sent:
+        move.wait_send()
 
 
 def score_kernel(parts_ref, refs_ref, out_ref, rolled, total):
@@ -91,46 +184,67 @@
     doms, groups = lax.axis_size("dom"), lax.axis_size("cls")
     devices = doms * groups
     width = pixels // devices
+    radii = width // ANGLES
     count = per_dev * devices
     classes = per_group * groups
-    everywhere = ("dom", "cls")
-
-    label = (group_ids[:, :, 0] * per_group + class_ids).astype(jnp.float32)
-    shift = (rot_ids * ASTEP).astype(jnp.float32)
-    meta = jnp.stack([label, shift, weights.astype(jnp.float32)])
-    flat = jnp.concatenate([meta.reshape(-1), prior_mass])
-    gathered = lax.all_gather(flat, everywhere, axis=0, tiled=False)
-    size = 3 * STEPS * per_dev
-    meta = gathered[:, :size].reshape(devices, 3, STEPS, per_dev).transpose(1, 2, 0, 3).reshape(3, STEPS, count)
-    prior = gathered[:groups, size:].reshape(classes, 1)
-
-    mine = lax.all_to_all(
-        particles.reshape(per_dev, devices, width).transpose(1, 0, 2), everywhere, split_axis=0, concat_axis=0, tiled=True
-    ).reshape(count, width)
+
+    meta = jnp.stack([group_ids[:, :, 0], class_ids, rot_ids]).astype(jnp.bfloat16)
+    meta = jnp.concatenate([meta, weights[None]]).reshape(-1)
+    size = meta.shape[0]
+    meta = jnp.pad(meta, (0, per_dev * ANGLES - size)).reshape(1, per_dev, ANGLES)
+    blocks = particles.reshape(per_dev, devices, radii, ANGLES).transpose(1, 2, 0, 3)
+    blocks = blocks.reshape(devices, radii * per_dev, ANGLES)
+    blocks = jnp.concatenate([blocks, jnp.broadcast_to(meta, (devices, per_dev, ANGLES))], axis=1)
+    mine = lax.all_to_all(blocks, ("dom", "cls"), split_axis=0, concat_axis=0, tiled=True)
+
     band = lax.dynamic_slice_in_dim(averages, lax.axis_index("dom") * groups * width, groups * width, 1)
-    band = lax.all_to_all(
-        band.reshape(per_group, groups, width).transpose(1, 0, 2), "cls", split_axis=0, concat_axis=0, tiled=True
-    ).reshape(classes, width)
+    band = band.reshape(per_group, groups, width).transpose(1, 0, 2)
+    extra = jnp.pad(prior_mass, (0, 8 * width - per_group)).reshape(1, 8, width)
+    band = jnp.concatenate([band, jnp.broadcast_to(extra, (groups, 8, width))], axis=1)
+    band = lax.all_to_all(band, "cls", split_axis=0, concat_axis=0, tiled=True)
+    prior = band[:, per_group, :per_group].reshape(classes, 1)
+
+    meta = mine[:, radii * per_dev :, :].reshape(devices, per_dev * ANGLES)[:, :size]
+    meta = meta.reshape(devices, 4, STEPS, per_dev).transpose(1, 2, 0, 3).reshape(4, STEPS, count).astype(jnp.float32)
+    label = (meta[0] * per_group + meta[1]).astype(jnp.int32)
+    shift = (meta[2] * ASTEP).astype(jnp.int32).T
 
     vmem = pl.BlockSpec(memory_space=pltpu.VMEM)
     refs, final = pl.pallas_call(
         update_kernel,
         out_shape=(
             jax.ShapeDtypeStruct((STEPS * per_group, width), jnp.bfloat16),
-            jax.ShapeDtypeStruct((classes, width), jnp.float32),
+            jax.ShapeDtypeStruct((groups, per_group, width), jnp.bfloat16),
         ),
         in_specs=[pl.BlockSpec(memory_space=pltpu.SMEM)] + [vmem] * 6,
         out_specs=(vmem, vmem),
+        scratch_shapes=[pltpu.VMEM((classes, width), jnp.float32)],
         compiler_params=pltpu.CompilerParams(vmem_limit_bytes=40 * MIB),
         name="update",
-    )(owners, mine, band, meta[0].astype(jnp.int32), meta[2], meta[1].astype(jnp.int32).T, prior)
-
-    all_refs = lax.all_gather(refs, everywhere, axis=0, tiled=False)
-    last = lax.all_to_all(
-        final.astype(jnp.bfloat16).reshape(groups, per_group, width), "cls", split_axis=0, concat_axis=0, tiled=True
-    )
-    last = lax.all_gather(last, "dom", axis=0, tiled=False)
-    last = last.transpose(2, 0, 1, 3).reshape(per_group, pixels).astype(jnp.float32)
+    )(owners, mine, band, label, meta[3], shift, prior)
+
+    hbm = pl.BlockSpec(memory_space=pl.ANY)
+    dma = pltpu.SemaphoreType.DMA
+    all_refs, last = pl.pallas_call(
+        functools.partial(gather_kernel, doms, groups),
+        out_shape=(
+            jax.ShapeDtypeStruct((doms, groups, STEPS * per_group, width), jnp.bfloat16),
+            jax.ShapeDtypeStruct((per_group, pixels), jnp.bfloat16),
+        ),
+        in_specs=[hbm, hbm],
+        out_specs=(hbm, hbm),
+        scratch_shapes=[
+            dma((2,)),
+            dma((2, groups)),
+            dma((2, groups)),
+            dma((2, 2, doms)),
+            dma((2, 2, doms)),
+        ],
+        compiler_params=pltpu.CompilerParams(collective_id=0, has_side_effects=True),
+        name="gather",
+    )(refs, final)
+    all_refs = all_refs.reshape(devices, STEPS * per_group, width)
+    last = last.astype(jnp.float32)
 
     chunks = 8
     scores = pl.pallas_call(

time: 205 us -> 119 us (0.58)
  the two profiles are of different devices: /device:TPU:0 before, /device:TPU:11 now
where the time goes in v2:
time: 119 us; the launch traced here: 118 us
  Pallas kernels  67.6 us (57%)
  waiting for transfers between devices  19.8 us (17%)
  local copies, waits for them, and re-layouts  14.1 us (12%)
  starting transfers between devices  12.3 us (10%)
  other arithmetic  3.75 us (3%)
    pallas_call x1, Pallas kernels, per_device(): pl.pallas_call(functools.partial(gather_kernel, doms, groups), out_shape=...  49.4 us
    pallas_call x1, Pallas kernels, per_device(): pl.pallas_call(score_kernel, grid=(chunks,), out_shape=jax.ShapeDtypeStru...  15.3 us
    all_to_all x1, waiting for transfers between devices, per_device(): lax.all_to_all(blocks, ('dom', 'cls'), split_axis=0, concat_axis=0, tiled...  14.8 us
    all_to_all x1, starting transfers between devices, per_device(): lax.all_to_all(blocks, ('dom', 'cls'), split_axis=0, concat_axis=0, tiled...  7.5 us
    unnamed x29, local copies, waits for them, and re-layouts  7.43 us
    all_to_all x1, waiting for transfers between devices, per_device(): band = lax.all_to_all(band, 'cls', split_axis=0, concat_axis=0, tiled=True)  4.99 us
    all_to_all x1, starting transfers between devices, per_device(): band = lax.all_to_all(band, 'cls', split_axis=0, concat_axis=0, tiled=True)  4.76 us
    pallas_call x1, Pallas kernels, per_device(): pl.pallas_call(update_kernel, out_shape=(jax.ShapeDtypeStruct((STEPS * pe...  2.93 us
  transfers between devices with their start and end apart: 2, of which 2 were waited for; matrix products, arithmetic and copies ran while one was open for 3% of the time, Pallas kernels for 0%

profile of v2, /device:TPU:11, one launch (start us, length us, event | category | flops | bytes accessed | tf_op | source)
XLA Modules:
  0.0 118.3 jit_solution(13782785323749461496)
XLA Ops:
  0.6 0.0 copy-start
  0.6 0.0 copy-start.12
  0.7 0.0 copy-start.10
  0.7 0.0 copy-start.11
  0.7 0.0 copy-start.13
  0.7 0.0 copy-start.2
  0.7 0.8 pad.9
  1.5 0.7 copy-done
  2.3 0.7 pad_maximum_fusion.1
  3.1 4.8 %all-to-all-start.1 = ((f32[4,40,512]{2,1,0:T(8,128)}), f32[4,40,512]{2,1,0:T(8,128)S(1)}, u32[]{:S(2)}, u32[]{:S(2)}) async-start(f32[4,40,512]{2,1,0:T(8,128)} %pad_maximum_fusion.1), calls=%async_computation.1 | async-start | bytes 655360 | tf_op jit(solution)/shard_map/all_to_all | solution.py:204
  7.8 0.0 copy-done.12
  7.8 0.0 copy-done.10
  7.8 0.0 copy-done.11
  7.9 0.0 copy-done.13
  7.9 0.1 reshape.53
  8.0 0.0 copy-done.2
  8.0 0.4 reshape.51
  8.4 0.6 copy.14
  9.0 0.9 pad_maximum_fusion
  9.9 5.0 %all-to-all-done.1.av_ref = f32[4,40,512]{2,1,0:T(8,128)S(1)} async-done(((f32[4,40,512]{2,1,0:T(8,128)}), f32[4,40,512]{2,1,0:T(8,128)S(1)}, u32[]{:S(2)}, u32[]{:S(2)}) %all-to-all-start.1) | async-done | bytes 327712 | tf_op jit(solution)/shard_map/all_to_all | solution.py:204
  14.9 0.0 copy-start.3
  14.9 0.7 copy-done.3
  15.6 7.5 %all-to-all-start = ((bf16[32,80,128]{2,1,0:T(8,128)(2,1)}), bf16[32,80,128]{2,1,0:T(8,128)(2,1)S(1)}, u32[]{:S(2)}, u32[]{:S(2)}) async-start(bf16[32,80,128]{2,1,0:T(8,128)(2,1)} %pad_maximum_fusion), calls=%async_computation | async-start | bytes 1310720 | tf_op jit(solution)/shard_map/all_to_all | solution.py:198
  23.1 0.7 slice_reduce_fusion
  23.9 0.7 reshape_squeeze.4.prior_ref
  24.6 14.8 %all-to-all-done.parts_ref = bf16[32,80,128]{2,1,0:T(8,128)(2,1)S(1)} async-done(((bf16[32,80,128]{2,1,0:T(8,128)(2,1)}), bf16[32,80,128]{2,1,0:T(8,128)(2,1)S(1)}, u32[]{:S(2)}, u32[]{:S(2)}) %all-to-all-start) | async-done | bytes 655392 | tf_op jit(solution)/shard_map/all_to_all | solution.py:198
  39.4 1.0 copy.21
  40.5 0.8 slice.33
  41.3 0.6 fusion
  42.0 0.1 copy.18
  42.0 0.1 squeeze.2.weight_ref
  42.1 0.1 copy.17
  42.2 0.1 convert_element_type.34.label_ref
  42.3 1.0 copy.19
  43.3 0.0 copy-start.4
  43.3 1.0 copy-done.4
  44.2 0.8 copy-done.5
  45.1 0.7 copy-done.8
  45.7 2.9 %update.1 = (bf16[128,512]{1,0:T(8,128)(2,1)S(1)}, bf16[4,32,512]{2,1,0:T(8,128)(2,1)S(1)}) custom-call(s32[4]{0:T(128)S(1)} %copy-done.8, bf16[32,80,128]{2,1,0:T(8,128)(2,1)S(1)} %all-to-all-done.parts_ref, f32[4,40,512]{2,1,0:T(8,128)S(1)} %copy-done.4, s32[4,512]{1,0:T(4,128)S(1)} %convert_element_type.34.label_ref, f32[4,512]{1,0:T(4,128)S(1)} %squeeze.2.weight_ref, ...), custom_call_target="tpu_custom_call" | custom-call | tf_op jit(solution)/shard_map/update/pallas_call | solution.py:213
  48.7 0.0 copy-start.6
  48.7 0.6 copy-done.6
  49.3 0.7 copy-done.7
  50.0 49.4 %gather.1 = (bf16[8,4,128,512]{3,2,1,0:T(8,128)(2,1)}, bf16[32,16384]{1,0:T(8,128)(2,1)}) custom-call(bf16[128,512]{1,0:T(8,128)(2,1)} %copy-done.6, bf16[4,32,512]{2,1,0:T(8,128)(2,1)} %copy-done.7), custom_call_target="tpu_custom_call" | custom-call | tf_op jit(solution)/shard_map/gather/pallas_call | solution.py:228
  99.4 0.0 copy-start.1
  99.4 2.2 %copy-done.1 = bf16[8,4,128,512]{3,2,1,0:T(8,128)(2,1)S(1)} copy-done((bf16[8,4,128,512]{3,2,1,0:T(8,128)(2,1)S(1)}, bf16[8,4,128,512]{3,2,1,0:T(8,128)(2,1)}, u32[]{:S(2)}) %copy-start.1) | copy-done | bytes 4194328
  101.5 15.3 %scores.1 = f32[4,16,2048]{2,1,0:T(8,128)} custom-call(bf16[16,16384]{1,0:T(8,128)(2,1)S(1)} %copy-done.2, bf16[32,128,512]{2,1,0:T(8,128)(2,1)S(1)} %bitcast.33), custom_call_target="tpu_custom_call" | custom-call | tf_op jit(solution)/shard_map/scores/pallas_call | solution.py:250
  116.8 0.0 copy-done.9
  116.8 1.5 %convert_element_type.37 = f32[32,16384]{1,0:T(8,128)} convert(bf16[32,16384]{1,0:T(8,128)(2,1)S(1)} %copy-done.9) | non-fusion elementwise | flops 524288 | bytes 3145728 | tf_op jit(solution)/shard_map/convert_element_type | solution.py:247
  (16 shorter events, 0.1 us)
Async XLA Ops:
  0.6 1.6 %copy-start = (f32[32,16384]{1,0:T(8,128)S(1)}, f32[32,16384]{1,0:T(8,128)}, u32[]{:S(2)}) copy-start(f32[32,16384]{1,0:T(8,128)} %param.9) | copy-start | bytes 6291460
  0.6 7.2 %copy-start.12 = (s32[4,16,1]{1,2,0:T(1,128)S(1)}, s32[4,16,1]{1,2,0:T(1,128)}, u32[]{:S(2)}) copy-start(s32[4,16,1]{1,2,0:T(1,128)} %param.11) | copy-start | bytes 772
  0.7 7.2 %copy-start.10 = (s32[4,16]{1,0:T(4,128)S(1)}, s32[4,16]{1,0:T(4,128)}, u32[]{:S(2)}) copy-start(s32[4,16]{1,0:T(4,128)} %param.13) | copy-start | bytes 772
  0.7 7.2 %copy-start.11 = (s32[4,16]{1,0:T(4,128)S(1)}, s32[4,16]{1,0:T(4,128)}, u32[]{:S(2)}) copy-start(s32[4,16]{1,0:T(4,128)} %param.12) | copy-start | bytes 772
  0.7 7.2 %copy-start.13 = (bf16[4,16]{1,0:T(4,128)(2,1)S(1)}, bf16[4,16]{1,0:T(4,128)(2,1)}, u32[]{:S(2)}) copy-start(bf16[4,16]{1,0:T(4,128)(2,1)} %param.14) | copy-start | bytes 388
  0.7 7.3 %copy-start.2 = (bf16[16,16384]{1,0:T(8,128)(2,1)S(1)}, bf16[16,16384]{1,0:T(8,128)(2,1)}, u32[]{:S(2)}) copy-start(bf16[16,16384]{1,0:T(8,128)(2,1)} %parts_ref.1) | copy-start | bytes 1572868
  3.1 11.8 %all-to-all-start.1 = ((f32[4,40,512]{2,1,0:T(8,128)}), f32[4,40,512]{2,1,0:T(8,128)S(1)}, u32[]{:S(2)}, u32[]{:S(2)}) async-start(f32[4,40,512]{2,1,0:T(8,128)} %pad_maximum_fusion.1), calls=%async_computation.1 | async-start | bytes 655360 | tf_op jit(solution)/shard_map/all_to_all | solution.py:204
  14.9 0.7 copy-start.3
  15.6 23.8 %all-to-all-start = ((bf16[32,80,128]{2,1,0:T(8,128)(2,1)}), bf16[32,80,128]{2,1,0:T(8,128)(2,1)S(1)}, u32[]{:S(2)}, u32[]{:S(2)}) async-start(bf16[32,80,128]{2,1,0:T(8,128)(2,1)} %pad_maximum_fusion), calls=%async_computation | async-start | bytes 1310720 | tf_op jit(solution)/shard_map/all_to_all | solution.py:198
  43.3 1.0 copy-start.4
  44.2 0.8 copy-start.5
  45.1 0.7 copy-start.8
  48.7 0.7 copy-start.6
  49.3 0.7 copy-start.7
  99.4 2.2 %copy-start.1 = (bf16[8,4,128,512]{3,2,1,0:T(8,128)(2,1)S(1)}, bf16[8,4,128,512]{3,2,1,0:T(8,128)(2,1)}, u32[]{:S(2)}) copy-start(bf16[8,4,128,512]{3,2,1,0:T(8,128)(2,1)} %get-tuple-element.8) | copy-start | bytes 12582916
  101.5 15.3 %copy-start.9 = (bf16[32,16384]{1,0:T(8,128)(2,1)S(1)}, bf16[32,16384]{1,0:T(8,128)(2,1)}, u32[]{:S(2)}) copy-start(bf16[32,16384]{1,0:T(8,128)(2,1)} %get-tuple-element.9) | copy-start | bytes 3145732

commit v3 on v2

--- a/solution.py
+++ b/solution.py
@@ -44,7 +44,73 @@
     last_ref[...] = current[...].astype(jnp.bfloat16).reshape(groups, per_group, width)
 
 
-def gather_kernel(doms, groups, refs_ref, final_ref, slots_ref, last_ref, own_sem, z_send, z_recv, d_send, d_recv):
+def exchange_kernel(doms, groups, blocks_ref, band_ref, mine_ref, got_ref, own_sem, send, recv, b_send, b_recv):
+    dom, cls = lax.axis_index("dom"), lax.axis_index("cls")
+    devices = doms * groups
+    me = dom * groups + cls
+
+    def peer(hop):
+        return lax.rem(me + hop, devices)
+
+    def place(device):
+        return {"dom": lax.div(device, groups), "cls": lax.rem(device, groups)}
+
+    barrier = pltpu.get_barrier_semaphore()
+
+    @pl.loop(1, devices)
+    def _(hop):
+        pl.semaphore_signal(barrier, device_id=place(peer(hop)), device_id_type=pl.DeviceIdType.MESH)
+
+    pl.semaphore_wait(barrier, devices - 1)
+
+    def block(hop):
+        return pltpu.make_async_remote_copy(
+            blocks_ref.at[peer(hop)],
+            mine_ref.at[me],
+            send.at[hop],
+            recv.at[hop],
+            place(peer(hop)),
+            pl.DeviceIdType.MESH,
+        )
+
+    def band(hop):
+        other = lax.rem(cls + hop, groups)
+        return pltpu.make_async_remote_copy(
+            band_ref.at[other],
+            got_ref.at[cls],
+            b_send.at[hop],
+            b_recv.at[hop],
+            {"dom": dom, "cls": other},
+            pl.DeviceIdType.MESH,
+        )
+
+    @pl.loop(1, devices)
+    def _(hop):
+        block(hop).start()
+
+    @pl.loop(1, groups)
+    def _(hop):
+        band(hop).start()
+
+    own = [
+        pltpu.make_async_copy(blocks_ref.at[me], mine_ref.at[me], own_sem.at[0]),
+        pltpu.make_async_copy(band_ref.at[cls], got_ref.at[cls], own_sem.at[1]),
+    ]
+    for copy in own:
+        copy.start()
+    for copy in own:
+        copy.wait()
+
+    @pl.loop(1, devices)
+    def _(hop):
+        block(hop).wait()
+
+    @pl.loop(1, groups)
+    def _(hop):
+        band(hop).wait()
+
+
+def gather_kernel(doms, groups, refs_ref, final_ref, slots_ref, last_ref, own_sem, z_send, z_recv, r_send, r_recv, f_send, f_recv):
     dom, cls = lax.axis_index("dom"), lax.axis_index("cls")
     bits = doms.bit_length() - 1
     per_group, width = final_ref.shape[1:]
@@ -65,17 +131,22 @@
     def columns(which_dom, which_cls, count):
         return pl.ds(pl.multiple_of((which_dom * groups + which_cls) * width, width), count * width)
 
+    half_rows = (refs_ref.shape[0] // 2, per_group // 2)
     own = [
         pltpu.make_async_copy(refs_ref, slots_ref.at[dom, cls], own_sem.at[0]),
         pltpu.make_async_copy(final_ref.at[cls], last_ref.at[:, columns(dom, cls, 1)], own_sem.at[1]),
     ]
-    sent = []
+    for copy in own:
+        copy.start()
+    z_refs, z_last = [], []
     for hop in range(1, groups):
         target = {"dom": dom, "cls": peer(hop)}
-        moves = [
+        z_refs.append(
             pltpu.make_async_remote_copy(
                 refs_ref, slots_ref.at[dom, cls], z_send.at[0, hop], z_recv.at[0, hop], target, pl.DeviceIdType.MESH
-            ),
+            )
+        )
+        z_last.append(
             pltpu.make_async_remote_copy(
                 final_ref.at[peer(hop)],
                 last_ref.at[:, columns(dom, cls, 1)],
@@ -83,55 +154,67 @@
                 z_recv.at[1, hop],
                 target,
                 pl.DeviceIdType.MESH,
-            ),
-        ]
+            )
+        )
+    for move in z_refs + z_last:
+        move.start()
+    for copy in own:
+        copy.wait()
+
+    orders = [list(range(1, bits)) + [0], list(range(bits - 1, 0, -1)) + [0]]
+
+    def begin(stage, piece_of, send_sem, recv_sem):
+        moves = []
+        for half, order in enumerate(orders):
+            target = {"dom": across(order[stage]), "cls": cls}
+            for pick in range(1 << stage):
+                slot = dom
+                for place, old in enumerate(order[:stage]):
+                    if pick >> place & 1:
+                        slot = slot + (1 << old) - (2 << old) * (lax.div(dom, 1 << old) % 2)
+                piece = piece_of(half, slot)
+                spot = (1 << stage) - 1 + pick
+                moves.append(
+                    pltpu.make_async_remote_copy(
+                        piece, piece, send_sem(half, spot), recv_sem(half, spot), target, pl.DeviceIdType.MESH
+                    )
+                )
         for move in moves:
             move.start()
-        sent.extend(moves)
-    for copy in own:
-        copy.start()
-    for copy in own:
-        copy.wait()
-    for move in sent:
-        move.wait_recv()
-
-    def part(half, which_dom):
-        span = groups // 2
-        rows = per_group // 2
-        return (
-            slots_ref.at[which_dom, half * span : (half + 1) * span],
-            last_ref.at[half * rows : (half + 1) * rows, columns(which_dom, 0, groups)],
-        )
-
-    orders = [list(range(1, bits)) + [0], list(range(bits - 1, 0, -1)) + [0]]
+        return moves
+
+    def refs_piece(source):
+        rows = half_rows[0]
+        return lambda half, slot: slots_ref.at[slot, source, half * rows : (half + 1) * rows]
+
+    def last_piece(half, slot):
+        rows = half_rows[1]
+        return last_ref.at[half * rows : (half + 1) * rows, columns(slot, 0, groups)]
+
+    sent = z_refs + z_last
+    flying = [[]] + [[move] for move in z_refs] + [z_last]
     for stage in range(bits):
-        moves = []
-        for half, order in enumerate(orders):
-            bit = order[stage]
-            done = order[:stage]
-            target = {"dom": across(bit), "cls": cls}
-            for pick in range(1 << stage):
-                slot = dom
-                for place, old in enumerate(done):
-                    if pick >> place & 1:
-                        slot = slot + (1 << old) - (2 << old) * (lax.div(dom, 1 << old) % 2)
-                for kind, piece in enumerate(part(half, slot)):
-                    spot = (1 << stage) - 1 + pick
-                    moves.append(
-                        pltpu.make_async_remote_copy(
-                            piece,
-                            piece,
-                            d_send.at[half, kind, spot],
-                            d_recv.at[half, kind, spot],
-                            target,
-                            pl.DeviceIdType.MESH,
-                        )
-                    )
-        for move in moves:
-            move.start()
+        for hop in range(groups + 1):
+            for move in flying[hop]:
+                move.wait_recv()
+            if hop < groups:
+                flying[hop] = begin(
+                    stage,
+                    refs_piece(lax.rem(cls + groups - hop, groups)),
+                    lambda half, spot: r_send.at[hop, half, spot],
+                    lambda half, spot: r_recv.at[hop, half, spot],
+                )
+            else:
+                flying[hop] = begin(
+                    stage,
+                    last_piece,
+                    lambda half, spot: f_send.at[half, spot],
+                    lambda half, spot: f_recv.at[half, spot],
+                )
+            sent.extend(flying[hop])
+    for moves in flying:
         for move in moves:
             move.wait_recv()
-        sent.extend(moves)
     for move in sent:
         move.wait_send()
 
@@ -195,13 +278,21 @@
     blocks = particles.reshape(per_dev, devices, radii, ANGLES).transpose(1, 2, 0, 3)
     blocks = blocks.reshape(devices, radii * per_dev, ANGLES)
     blocks = jnp.concatenate([blocks, jnp.broadcast_to(meta, (devices, per_dev, ANGLES))], axis=1)
-    mine = lax.all_to_all(blocks, ("dom", "cls"), split_axis=0, concat_axis=0, tiled=True)
-
     band = lax.dynamic_slice_in_dim(averages, lax.axis_index("dom") * groups * width, groups * width, 1)
     band = band.reshape(per_group, groups, width).transpose(1, 0, 2)
     extra = jnp.pad(prior_mass, (0, 8 * width - per_group)).reshape(1, 8, width)
     band = jnp.concatenate([band, jnp.broadcast_to(extra, (groups, 8, width))], axis=1)
-    band = lax.all_to_all(band, "cls", split_axis=0, concat_axis=0, tiled=True)
+    hbm = pl.BlockSpec(memory_space=pl.ANY)
+    dma = pltpu.SemaphoreType.DMA
+    mine, band = pl.pallas_call(
+        functools.partial(exchange_kernel, doms, groups),
+        out_shape=(jax.ShapeDtypeStruct(blocks.shape, blocks.dtype), jax.ShapeDtypeStruct(band.shape, band.dtype)),
+        in_specs=[hbm, hbm],
+        out_specs=(hbm, hbm),
+        scratch_shapes=[dma((2,)), dma((devices,)), dma((devices,)), dma((groups,)), dma((groups,))],
+        compiler_params=pltpu.CompilerParams(collective_id=1, has_side_effects=True),
+        name="exchange",
+    )(blocks, band)
     prior = band[:, per_group, :per_group].reshape(classes, 1)
 
     meta = mine[:, radii * per_dev :, :].reshape(devices, per_dev * ANGLES)[:, :size]
@@ -223,8 +314,6 @@
         name="update",
     )(owners, mine, band, label, meta[3], shift, prior)
 
-    hbm = pl.BlockSpec(memory_space=pl.ANY)
-    dma = pltpu.SemaphoreType.DMA
     all_refs, last = pl.pallas_call(
         functools.partial(gather_kernel, doms, groups),
         out_shape=(
@@ -237,8 +326,10 @@
             dma((2,)),
             dma((2, groups)),
             dma((2, groups)),
-            dma((2, 2, doms)),
-            dma((2, 2, doms)),
+            dma((groups, 2, doms)),
+            dma((groups, 2, doms)),
+            dma((2, doms)),
+            dma((2, doms)),
         ],
         compiler_params=pltpu.CompilerParams(collective_id=0, has_side_effects=True),
         name="gather",

time: 119 us -> 106 us (0.89)
  the two profiles are of different devices: /device:TPU:11 before, /device:TPU:0 now
where the time goes in v3:
time: 106 us
  Pallas kernels  85.4 us (81%)
  local copies, waits for them, and re-layouts  13.4 us (13%)
  other arithmetic  5.95 us (6%)
    pallas_call x1, Pallas kernels, per_device(): pl.pallas_call(functools.partial(gather_kernel, doms, groups), out_shape=...  38.3 us
    pallas_call x1, Pallas kernels, per_device(): pl.pallas_call(functools.partial(exchange_kernel, doms, groups), out_shap...  28.9 us
    pallas_call x1, Pallas kernels, per_device(): pl.pallas_call(score_kernel, grid=(chunks,), out_shape=jax.ShapeDtypeStru...  15.3 us
    unnamed x21, local copies, waits for them, and re-layouts  5.97 us
    pallas_call x1, Pallas kernels, per_device(): pl.pallas_call(update_kernel, out_shape=(jax.ShapeDtypeStruct((STEPS * pe...  2.93 us

profile of v3, /device:TPU:0, one launch (start us, length us, event | category | flops | bytes accessed | tf_op | source)
XLA Modules:
  0.0 105.6 jit_solution(4438407501473942335)
XLA Ops:
  0.6 0.0 copy-start
  0.6 0.0 copy-start.2
  0.7 0.8 convert.14
  1.5 0.7 convert_bitcast_fusion.1
  2.2 0.7 pad_maximum_fusion.2
  2.9 0.1 reshape.53
  3.0 0.7 pad.9
  3.7 0.0 copy-done
  3.8 0.7 pad_maximum_fusion.1.band_ref
  4.5 0.0 copy-done.2
  4.5 0.4 reshape.51
  4.9 0.6 copy.14
  5.5 0.9 pad_maximum_fusion.blocks_ref
  6.4 28.9 %exchange.1 = (bf16[32,80,128]{2,1,0:T(8,128)(2,1)}, f32[4,40,512]{2,1,0:T(8,128)}) custom-call(bf16[32,80,128]{2,1,0:T(8,128)(2,1)} %pad_maximum_fusion.blocks_ref, f32[4,40,512]{2,1,0:T(8,128)} %pad_maximum_fusion.1.band_ref), custom_call_target="tpu_custom_call" | custom-call | tf_op jit(solution)/shard_map/exchange/pallas_call | solution.py:287
  35.3 0.0 copy-start.3
  35.3 0.8 slice_reduce_fusion
  36.1 0.7 reshape_squeeze.4.prior_ref
  36.8 0.9 slice.25
  37.8 1.0 copy.21
  38.8 0.8 slice.32
  39.7 0.6 fusion
  40.3 0.1 copy.18
  40.4 0.1 squeeze.2.weight_ref
  40.5 0.1 copy.17
  40.5 0.1 convert_element_type.34.label_ref
  40.6 1.0 copy.19
  41.6 0.0 copy-done.3
  41.6 0.0 copy-start.4
  41.6 1.0 copy-done.4
  42.6 0.0 copy-start.5
  42.6 0.8 copy-done.5
  43.4 0.0 copy-start.8
  43.4 0.7 copy-done.8
  44.1 2.9 %update.1 = (bf16[128,512]{1,0:T(8,128)(2,1)S(1)}, bf16[4,32,512]{2,1,0:T(8,128)(2,1)S(1)}) custom-call(s32[4]{0:T(128)S(1)} %copy-done.8, bf16[32,80,128]{2,1,0:T(8,128)(2,1)S(1)} %copy-done.3, f32[4,40,512]{2,1,0:T(8,128)S(1)} %copy-done.4, s32[4,512]{1,0:T(4,128)S(1)} %convert_element_type.34.label_ref, f32[4,512]{1,0:T(4,128)S(1)} %squeeze.2.weight_ref, ...), custom_call_target="tpu_custom_call" | custom-call | tf_op jit(solution)/shard_map/update/pallas_call | solution.py:304
  47.0 0.0 copy-start.6
  47.0 0.6 copy-done.6
  47.7 0.0 copy-start.7
  47.7 0.7 copy-done.7
  48.3 38.3 %gather.1 = (bf16[8,4,128,512]{3,2,1,0:T(8,128)(2,1)}, bf16[32,16384]{1,0:T(8,128)(2,1)}) custom-call(bf16[128,512]{1,0:T(8,128)(2,1)} %copy-done.6, bf16[4,32,512]{2,1,0:T(8,128)(2,1)} %copy-done.7), custom_call_target="tpu_custom_call" | custom-call | tf_op jit(solution)/shard_map/gather/pallas_call | solution.py:317
  86.6 0.0 copy-start.1
  86.7 2.2 %copy-done.1 = bf16[8,4,128,512]{3,2,1,0:T(8,128)(2,1)S(1)} copy-done((bf16[8,4,128,512]{3,2,1,0:T(8,128)(2,1)S(1)}, bf16[8,4,128,512]{3,2,1,0:T(8,128)(2,1)}, u32[]{:S(2)}) %copy-start.1) | copy-done | bytes 4194328
  88.8 0.0 copy-start.9
  88.8 15.3 %scores.1 = f32[4,16,2048]{2,1,0:T(8,128)} custom-call(bf16[16,16384]{1,0:T(8,128)(2,1)S(1)} %copy-done.2, bf16[32,128,512]{2,1,0:T(8,128)(2,1)S(1)} %bitcast.33), custom_call_target="tpu_custom_call" | custom-call | tf_op jit(solution)/shard_map/scores/pallas_call | solution.py:341
  104.1 0.0 copy-done.9
  104.1 1.5 %convert_element_type.37 = f32[32,16384]{1,0:T(8,128)} convert(bf16[32,16384]{1,0:T(8,128)(2,1)S(1)} %copy-done.9) | non-fusion elementwise | flops 524288 | bytes 3145728 | tf_op jit(solution)/shard_map/convert_element_type | solution.py:338
  (8 shorter events, 0.1 us)
Async XLA Ops:
  0.6 3.1 %copy-start = (f32[32,16384]{1,0:T(8,128)S(1)}, f32[32,16384]{1,0:T(8,128)}, u32[]{:S(2)}) copy-start(f32[32,16384]{1,0:T(8,128)} %param.9) | copy-start | bytes 6291460
  0.6 3.9 %copy-start.2 = (bf16[16,16384]{1,0:T(8,128)(2,1)S(1)}, bf16[16,16384]{1,0:T(8,128)(2,1)}, u32[]{:S(2)}) copy-start(bf16[16,16384]{1,0:T(8,128)(2,1)} %parts_ref.1) | copy-start | bytes 1572868
  35.3 6.3 %copy-start.3 = (bf16[32,80,128]{2,1,0:T(8,128)(2,1)S(1)}, bf16[32,80,128]{2,1,0:T(8,128)(2,1)}, u32[]{:S(2)}) copy-start(bf16[32,80,128]{2,1,0:T(8,128)(2,1)} %get-tuple-element.8.parts_ref) | copy-start | bytes 1966084
  41.6 1.0 copy-start.4
  42.6 0.8 copy-start.5
  43.4 0.7 copy-start.8
  47.0 0.7 copy-start.6
  47.7 0.7 copy-start.7
  86.6 2.2 %copy-start.1 = (bf16[8,4,128,512]{3,2,1,0:T(8,128)(2,1)S(1)}, bf16[8,4,128,512]{3,2,1,0:T(8,128)(2,1)}, u32[]{:S(2)}) copy-start(bf16[8,4,128,512]{3,2,1,0:T(8,128)(2,1)} %get-tuple-element.12) | copy-start | bytes 12582916
  88.8 15.3 %copy-start.9 = (bf16[32,16384]{1,0:T(8,128)(2,1)S(1)}, bf16[32,16384]{1,0:T(8,128)(2,1)}, u32[]{:S(2)}) copy-start(bf16[32,16384]{1,0:T(8,128)(2,1)} %get-tuple-element.13) | copy-start | bytes 3145732

commit v4 on v3

--- a/solution.py
+++ b/solution.py
@@ -16,29 +16,38 @@
 MIB = 1024 * 1024
 
 
-def update_kernel(owners_ref, parts_ref, av_ref, label_ref, weight_ref, shift_ref, prior_ref, refs_ref, last_ref, current):
+def update_kernel(owners_ref, parts_ref, av_ref, refs_ref, last_ref, current):
     senders, rows = parts_ref.shape[:2]
-    groups, padded, width = av_ref.shape
-    per_group = last_ref.shape[1]
+    groups, per_group, wide = av_ref.shape
+    width = wide - ANGLES
     radii = width // ANGLES
     per_dev = rows // (radii + 1)
     count, classes = senders * per_dev, groups * per_group
-    prior = prior_ref[...]
+    prior = av_ref[:, :, width:].reshape(classes, ANGLES)
+    meta = parts_ref[:, radii * per_dev :, :].reshape(count, ANGLES).astype(jnp.float32)
     lane = lax.broadcasted_iota(jnp.int32, (count, ANGLES), 1)
-    class_row = lax.broadcasted_iota(jnp.int32, (classes, count), 0)
-    current[...] = av_ref[:, :per_group, :].reshape(classes, width)
+    class_lane = lax.broadcasted_iota(jnp.int32, (count, classes), 1)
+    ones = jnp.ones((count, ANGLES), jnp.bfloat16)
+    current[...] = av_ref[:, :, :width].reshape(classes, width)
+
+    def value(kind, step):
+        return meta[:, kind * STEPS + step : kind * STEPS + step + 1]
+
     for step in range(STEPS):
-        index = (lane - shift_ref[:, step : step + 1]) & (ANGLES - 1)
-        hot = jnp.where(class_row == label_ref[step : step + 1, :], weight_ref[step : step + 1, :], 0.0)
-        mass = jnp.sum(hot, axis=1, keepdims=True)
-        hot = hot.astype(jnp.bfloat16)
-        inverse = 1.0 / (prior + mass)
+        shift = (value(2, step) * ASTEP).astype(jnp.int32)
+        label = (value(0, step) * per_group + value(1, step)).astype(jnp.int32)
+        index = (lane - shift) & (ANGLES - 1)
+        hot = jnp.where(class_lane == label, value(3, step), 0.0).astype(jnp.bfloat16)
+
+        def summed(values):
+            return lax.dot_general(hot, values, (((0,), (0,)), ((), ())), preferred_element_type=jnp.float32)
+
+        inverse = 1.0 / (prior + summed(ones))
         for a in range(radii):
             cols = slice(a * ANGLES, (a + 1) * ANGLES)
             image = parts_ref[:, a * per_dev : (a + 1) * per_dev, :].reshape(count, ANGLES).astype(jnp.float32)
             turned = jnp.take_along_axis(image, index, axis=1).astype(jnp.bfloat16)
-            totals = jnp.dot(hot, turned, preferred_element_type=jnp.float32)
-            current[:, cols] = (prior * current[:, cols] + totals) * inverse
+            current[:, cols] = (prior * current[:, cols] + summed(turned)) * inverse
         start = pl.multiple_of(owners_ref[step] * per_group, per_group)
         refs_ref[step * per_group : (step + 1) * per_group, :] = current[pl.ds(start, per_group), :].astype(jnp.bfloat16)
     last_ref[...] = current[...].astype(jnp.bfloat16).reshape(groups, per_group, width)
@@ -110,7 +119,25 @@
         band(hop).wait()
 
 
-def gather_kernel(doms, groups, refs_ref, final_ref, slots_ref, last_ref, own_sem, z_send, z_recv, r_send, r_recv, f_send, f_recv):
+def gather_kernel(
+    doms,
+    groups,
+    refs_ref,
+    final_ref,
+    images_ref,
+    last_ref,
+    scores_ref,
+    slots_ref,
+    rolled,
+    total,
+    own_sem,
+    z_send,
+    z_recv,
+    r_send,
+    r_recv,
+    f_send,
+    f_recv,
+):
     dom, cls = lax.axis_index("dom"), lax.axis_index("cls")
     bits = doms.bit_length() - 1
     per_group, width = final_ref.shape[1:]
@@ -191,6 +218,31 @@
         rows = half_rows[1]
         return last_ref.at[half * rows : (half + 1) * rows, columns(slot, 0, groups)]
 
+    radii = width // ANGLES
+    per_dev = images_ref.shape[1]
+    chunks = 8
+    depth = images_ref.shape[0] // chunks
+
+    def roll_chunk(chunk):
+        part = slice(chunk * depth, (chunk + 1) * depth)
+        images = images_ref[part].reshape(depth * per_dev, ANGLES)
+        for r in range(ROT):
+            turned = pltpu.roll(images, r * ASTEP, 1) if r else images
+            rolled[part, r * per_dev : (r + 1) * per_dev, :] = turned.reshape(depth, per_dev, ANGLES)
+
+    def multiply(source, core):
+        @pl.loop(0, doms // 2)
+        def _(pair):
+            which = 2 * pair + core
+            base = (which * groups + source) * radii
+            views = jnp.concatenate([rolled[base + j] for j in range(radii)], axis=1)
+            total[...] += lax.dot_general(
+                views, slots_ref[which, source], (((1,), (1,)), ((), ())), preferred_element_type=jnp.float32
+            )
+
+    total[...] = jnp.zeros_like(total)
+    todo = list(range(chunks))
+    core = lax.rem(dom, 2)
     sent = z_refs + z_last
     flying = [[]] + [[move] for move in z_refs] + [z_last]
     for stage in range(bits):
@@ -198,9 +250,10 @@
             for move in flying[hop]:
                 move.wait_recv()
             if hop < groups:
+                source = lax.rem(cls + groups - hop, groups)
                 flying[hop] = begin(
                     stage,
-                    refs_piece(lax.rem(cls + groups - hop, groups)),
+                    refs_piece(source),
                     lambda half, spot: r_send.at[hop, half, spot],
                     lambda half, spot: r_recv.at[hop, half, spot],
                 )
@@ -212,53 +265,32 @@
                     lambda half, spot: f_recv.at[half, spot],
                 )
             sent.extend(flying[hop])
-    for moves in flying:
-        for move in moves:
+            if stage == bits - 1:
+                for chunk in todo:
+                    roll_chunk(chunk)
+                todo = []
+                if hop < groups:
+                    multiply(source, core)
+            elif hop < groups:
+                for chunk in todo[: 2 if stage == hop == 0 else 1]:
+                    roll_chunk(chunk)
+                todo = todo[2 if stage == hop == 0 else 1 :]
+    for hop in range(groups + 1):
+        for move in flying[hop]:
             move.wait_recv()
+        if hop < groups:
+            multiply(lax.rem(cls + groups - hop, groups), 1 - core)
+
+    scale = 1.0 / math.sqrt(RADII * ANGLES)
+    pack = ANGLES // per_group
+    for q in range(ROT // pack):
+        tiles = [total[(q * pack + j) * per_dev : (q * pack + j + 1) * per_dev, :] * scale for j in range(pack)]
+        for s in range(STEPS):
+            scores_ref[s, :, q * ANGLES : (q + 1) * ANGLES] = jnp.concatenate(
+                [t[:, s * per_group : (s + 1) * per_group] for t in tiles], axis=1
+            )
     for move in sent:
         move.wait_send()
-
-
-def score_kernel(parts_ref, refs_ref, out_ref, rolled, total):
-    step = pl.program_id(0)
-    per_dev = parts_ref.shape[0]
-    blocks, names, width = refs_ref.shape
-    per_group = names // STEPS
-    radii = parts_ref.shape[1] // ANGLES
-    for a in range(radii):
-        cols = slice(a * ANGLES, (a + 1) * ANGLES)
-        image = parts_ref[:, cols]
-        for r in range(ROT):
-            turned = pltpu.roll(image, r * ASTEP, 1) if r else image
-            rolled[r * per_dev : (r + 1) * per_dev, cols] = turned
-    product = None
-    for b in range(blocks):
-        part = lax.dot_general(
-            rolled[:, b * width : (b + 1) * width],
-            refs_ref[b],
-            (((1,), (1,)), ((), ())),
-            preferred_element_type=jnp.float32,
-        )
-        product = part if product is None else product + part
-
-    @pl.when(step == 0)
-    def _():
-        total[...] = product
-
-    @pl.when(step > 0)
-    def _():
-        total[...] += product
-
-    @pl.when(step == pl.num_programs(0) - 1)
-    def _():
-        scale = 1.0 / math.sqrt(RADII * ANGLES)
-        pack = 128 // per_group
-        for q in range(ROT // pack):
-            tiles = [total[(q * pack + j) * per_dev : (q * pack + j + 1) * per_dev, :] * scale for j in range(pack)]
-            for s in range(STEPS):
-                out_ref[s, :, q * 128 : (q + 1) * 128] = jnp.concatenate(
-                    [t[:, s * per_group : (s + 1) * per_group] for t in tiles], axis=1
-                )
 
 
 def per_device(particles, averages, prior_mass, group_ids, class_ids, rot_ids, weights, owners):
@@ -268,20 +300,18 @@
     devices = doms * groups
     width = pixels // devices
     radii = width // ANGLES
-    count = per_dev * devices
     classes = per_group * groups
 
     meta = jnp.stack([group_ids[:, :, 0], class_ids, rot_ids]).astype(jnp.bfloat16)
-    meta = jnp.concatenate([meta, weights[None]]).reshape(-1)
-    size = meta.shape[0]
-    meta = jnp.pad(meta, (0, per_dev * ANGLES - size)).reshape(1, per_dev, ANGLES)
-    blocks = particles.reshape(per_dev, devices, radii, ANGLES).transpose(1, 2, 0, 3)
-    blocks = blocks.reshape(devices, radii * per_dev, ANGLES)
+    meta = jnp.concatenate([meta, weights[None]]).reshape(4 * STEPS, per_dev).T
+    meta = jnp.pad(meta, ((0, 0), (0, ANGLES - 4 * STEPS)))[None]
+    images = particles.reshape(per_dev, pixels // ANGLES, ANGLES).transpose(1, 0, 2)
+    blocks = images.reshape(devices, radii * per_dev, ANGLES)
     blocks = jnp.concatenate([blocks, jnp.broadcast_to(meta, (devices, per_dev, ANGLES))], axis=1)
     band = lax.dynamic_slice_in_dim(averages, lax.axis_index("dom") * groups * width, groups * width, 1)
     band = band.reshape(per_group, groups, width).transpose(1, 0, 2)
-    extra = jnp.pad(prior_mass, (0, 8 * width - per_group)).reshape(1, 8, width)
-    band = jnp.concatenate([band, jnp.broadcast_to(extra, (groups, 8, width))], axis=1)
+    extra = jnp.broadcast_to(prior_mass[None, :, None], (groups, per_group, ANGLES))
+    band = jnp.concatenate([band, extra], axis=2)
     hbm = pl.BlockSpec(memory_space=pl.ANY)
     dma = pltpu.SemaphoreType.DMA
     mine, band = pl.pallas_call(
@@ -293,13 +323,6 @@
         compiler_params=pltpu.CompilerParams(collective_id=1, has_side_effects=True),
         name="exchange",
     )(blocks, band)
-    prior = band[:, per_group, :per_group].reshape(classes, 1)
-
-    meta = mine[:, radii * per_dev :, :].reshape(devices, per_dev * ANGLES)[:, :size]
-    meta = meta.reshape(devices, 4, STEPS, per_dev).transpose(1, 2, 0, 3).reshape(4, STEPS, count).astype(jnp.float32)
-    label = (meta[0] * per_group + meta[1]).astype(jnp.int32)
-    shift = (meta[2] * ASTEP).astype(jnp.int32).T
-
     vmem = pl.BlockSpec(memory_space=pltpu.VMEM)
     refs, final = pl.pallas_call(
         update_kernel,
@@ -307,22 +330,25 @@
             jax.ShapeDtypeStruct((STEPS * per_group, width), jnp.bfloat16),
             jax.ShapeDtypeStruct((groups, per_group, width), jnp.bfloat16),
         ),
-        in_specs=[pl.BlockSpec(memory_space=pltpu.SMEM)] + [vmem] * 6,
+        in_specs=[pl.BlockSpec(memory_space=pltpu.SMEM)] + [vmem] * 2,
         out_specs=(vmem, vmem),
         scratch_shapes=[pltpu.VMEM((classes, width), jnp.float32)],
         compiler_params=pltpu.CompilerParams(vmem_limit_bytes=40 * MIB),
         name="update",
-    )(owners, mine, band, label, meta[3], shift, prior)
-
-    all_refs, last = pl.pallas_call(
+    )(owners, mine, band)
+
+    last, scores = pl.pallas_call(
         functools.partial(gather_kernel, doms, groups),
         out_shape=(
-            jax.ShapeDtypeStruct((doms, groups, STEPS * per_group, width), jnp.bfloat16),
             jax.ShapeDtypeStruct((per_group, pixels), jnp.bfloat16),
+            jax.ShapeDtypeStruct((STEPS, per_dev, ROT * per_group), jnp.float32),
         ),
-        in_specs=[hbm, hbm],
-        out_specs=(hbm, hbm),
+        in_specs=[hbm, hbm, vmem],
+        out_specs=(hbm, vmem),
         scratch_shapes=[
+            pltpu.VMEM((doms, groups, STEPS * per_group, width), jnp.bfloat16),
+            pltpu.VMEM((pixels // ANGLES, ROT * per_dev, ANGLES), jnp.bfloat16),
+            pltpu.VMEM((ROT * per_dev, STEPS * per_group), jnp.float32),
             dma((2,)),
             dma((2, groups)),
             dma((2, groups)),
@@ -331,30 +357,12 @@
             dma((2, doms)),
             dma((2, doms)),
         ],
-        compiler_params=pltpu.CompilerParams(collective_id=0, has_side_effects=True),
-        name="gather",
-    )(refs, final)
-    all_refs = all_refs.reshape(devices, STEPS * per_group, width)
-    last = last.astype(jnp.float32)
-
-    chunks = 8
-    scores = pl.pallas_call(
-        score_kernel,
-        grid=(chunks,),
-        out_shape=jax.ShapeDtypeStruct((STEPS, per_dev, ROT * per_group), jnp.float32),
-        in_specs=[
-            pl.BlockSpec((per_dev, pixels // chunks), lambda c: (0, c)),
-            pl.BlockSpec((devices // chunks, STEPS * per_group, width), lambda c: (c, 0, 0)),
-        ],
-        out_specs=pl.BlockSpec((STEPS, per_dev, ROT * per_group), lambda c: (0, 0, 0)),
-        scratch_shapes=[
-            pltpu.VMEM((ROT * per_dev, pixels // chunks), jnp.bfloat16),
-            pltpu.VMEM((ROT * per_dev, STEPS * per_group), jnp.float32),
-        ],
-        compiler_params=pltpu.CompilerParams(vmem_limit_bytes=40 * MIB),
-        name="scores",
-    )(particles, all_refs)
-    return scores, last
+        compiler_params=pltpu.CompilerParams(
+            collective_id=0, has_side_effects=True, vmem_limit_bytes=52 * MIB
+        ),
+        name="gather_scores",
+    )(refs, final, images)
+    return scores, last.astype(jnp.float32)
 
 
 def solution(mesh):

time: 106 us -> 88.3 us (0.83)
  local copies, waits for them, and re-layouts: 13.4 us -> 3.89 us
  Pallas kernels: 85.4 us -> 76.9 us
    pallas_call x1 -> x0, Pallas kernels: 15.3 us -> none  [per_device(): pl.pallas_call(score_kernel, grid=(chunks,), out_shape=jax.ShapeDtypeStru...]
    pallas_call x1, Pallas kernels: 38.3 us -> 44.5 us  [per_device(): pl.pallas_call(functools.partial(gather_kernel, doms, groups), out_shape=...]
    unnamed x21 -> x12, local copies, waits for them, and re-layouts: 5.97 us -> 2.87 us
    slice x4 -> x0, local copies, waits for them, and re-layouts: 2.64 us -> none  [the longest x2 1.76 us: per_device(): mine[:, radii * per_dev:, :].reshape(devices, per_dev * ANGLES)[:, :size]]
    reshape x4 -> x1, local copies, waits for them, and re-layouts: 2.11 us -> 0.08 us  [per_device(): meta = jnp.concatenate([meta, weights[None]]).reshape(4 * STEPS, per_dev).T]
    convert_element_type x3 -> x0, local copies, waits for them, and re-layouts: 1.13 us -> none  [the longest x1 0.95 us: per_device(): shift = (meta[2] * ASTEP).astype(jnp.int32).T]
    convert_element_type x3 -> x1, other arithmetic: 2.09 us -> 2.68 us  [per_device(): return (scores, last.astype(jnp.float32))]
where the time goes in v4:
time: 88.3 us; the launch traced here: 88 us
  Pallas kernels  76.9 us (87%)
  other arithmetic  6.54 us (7%)
  local copies, waits for them, and re-layouts  3.89 us (4%)
    pallas_call x1, Pallas kernels, per_device(): pl.pallas_call(functools.partial(gather_kernel, doms, groups), out_shape=...  44.5 us
    pallas_call x1, Pallas kernels, per_device(): pl.pallas_call(functools.partial(exchange_kernel, doms, groups), out_shap...  28.9 us
    pallas_call x1, Pallas kernels, per_device(): pl.pallas_call(update_kernel, out_shape=(jax.ShapeDtypeStruct((STEPS * pe...  3.53 us
    unnamed x12, local copies, waits for them, and re-layouts  2.87 us
    convert_element_type x1, other arithmetic, per_device(): return (scores, last.astype(jnp.float32))  2.68 us

profile of v4, /device:TPU:0, one launch (start us, length us, event | category | flops | bytes accessed | tf_op | source)
XLA Modules:
  0.0 88.0 jit_solution(177447060195803005)
XLA Ops:
  0.6 0.0 copy-start
  0.6 0.0 copy-start.4
  0.7 0.8 convert.12
  1.5 0.7 convert_bitcast_fusion
  2.2 0.7 pad_maximum_fusion.2
  2.9 0.1 copy.12
  3.0 0.7 broadcast_in_dim.8
  3.7 0.0 copy-done
  3.8 0.8 pad_maximum_fusion.1.band_ref
  4.6 0.0 copy-done.4
  4.6 0.0 copy-start.3
  4.6 0.1 fusion
  4.7 0.9 %pad_maximum_fusion.blocks_ref = bf16[32,80,128]{2,1,0:T(8,128)(2,1)} fusion(bf16[32,16,128]{2,1,0:T(8,128)(2,1)S(1)} %broadcast_in_dim.7, bf16[32,64,128]{2,1,0:T(8,128)(2,1)S(1)} %bitcast.28), kind=kLoop, calls=%fused_computation | loop fusion | flops 1310720 | bytes 1310720 | tf_op jit(solution)/shard_map/concatenate | solution.py:310
  5.6 28.9 %exchange.1 = (bf16[32,80,128]{2,1,0:T(8,128)(2,1)}, f32[4,32,640]{2,1,0:T(8,128)}) custom-call(bf16[32,80,128]{2,1,0:T(8,128)(2,1)} %pad_maximum_fusion.blocks_ref, f32[4,32,640]{2,1,0:T(8,128)} %pad_maximum_fusion.1.band_ref), custom_call_target="tpu_custom_call" | custom-call | tf_op jit(solution)/shard_map/exchange/pallas_call | solution.py:317
  34.5 0.0 copy-done.3
  34.5 0.0 copy-start.1
  34.5 1.1 %copy-done.1 = bf16[32,80,128]{2,1,0:T(8,128)(2,1)S(1)} copy-done((bf16[32,80,128]{2,1,0:T(8,128)(2,1)S(1)}, bf16[32,80,128]{2,1,0:T(8,128)(2,1)}, u32[]{:S(2)}) %copy-start.1) | copy-done | bytes 655384
  35.6 0.0 copy-start.2
  35.6 1.0 %copy-done.2 = f32[4,32,640]{2,1,0:T(8,128)S(1)} copy-done((f32[4,32,640]{2,1,0:T(8,128)S(1)}, f32[4,32,640]{2,1,0:T(8,128)}, u32[]{:S(2)}) %copy-start.2) | copy-done | bytes 327704
  36.6 3.5 %update.1 = (bf16[128,512]{1,0:T(8,128)(2,1)S(1)}, bf16[4,32,512]{2,1,0:T(8,128)(2,1)S(1)}) custom-call(s32[4]{0:T(128)S(1)} %copy-done.3, bf16[32,80,128]{2,1,0:T(8,128)(2,1)S(1)} %copy-done.1, f32[4,32,640]{2,1,0:T(8,128)S(1)} %copy-done.2), custom_call_target="tpu_custom_call" | custom-call | tf_op jit(solution)/shard_map/update/pallas_call | solution.py:327
  40.1 44.5 %gather_scores.1 = (bf16[32,16384]{1,0:T(8,128)(2,1)}, f32[4,16,2048]{2,1,0:T(8,128)S(1)}) custom-call(bf16[128,512]{1,0:T(8,128)(2,1)S(1)} %get-tuple-element.10.refs_ref, bf16[4,32,512]{2,1,0:T(8,128)(2,1)S(1)} %get-tuple-element.11.final_ref, bf16[128,16,128]{2,1,0:T(8,128)(2,1)S(1)} %get-tuple-element.14.images_ref), custom_call_target="tpu_custom_call" | custom-call | tf_op jit(solution)/shard_map/gather_scores/pallas_call | solution.py:340
  84.5 2.7 %convert_element_type.6 = f32[32,16384]{1,0:T(8,128)} convert(bf16[32,16384]{1,0:T(8,128)(2,1)} %get-tuple-element.13) | non-fusion elementwise | flops 524288 | bytes 3145728 | tf_op jit(solution)/shard_map/convert_element_type | solution.py:365
  87.2 0.8 copy.25
  (5 shorter events, 0.1 us)
Async XLA Ops:
  0.6 3.1 %copy-start = (f32[32,16384]{1,0:T(8,128)S(1)}, f32[32,16384]{1,0:T(8,128)}, u32[]{:S(2)}) copy-start(f32[32,16384]{1,0:T(8,128)} %param.9) | copy-start | bytes 6291460
  0.6 3.9 %copy-start.4 = (bf16[16,16384]{1,0:T(8,128)(2,1)S(1)}, bf16[16,16384]{1,0:T(8,128)(2,1)}, u32[]{:S(2)}) copy-start(bf16[16,16384]{1,0:T(8,128)(2,1)} %param.8) | copy-start | bytes 1572868
  4.6 29.9 %copy-start.3 = (s32[4]{0:T(128)S(1)}, s32[4]{0:T(128)}, u32[]{:S(2)}) copy-start(s32[4]{0:T(128)} %owners_ref.1) | copy-start | bytes 52
  34.5 1.1 %copy-start.1 = (bf16[32,80,128]{2,1,0:T(8,128)(2,1)S(1)}, bf16[32,80,128]{2,1,0:T(8,128)(2,1)}, u32[]{:S(2)}) copy-start(bf16[32,80,128]{2,1,0:T(8,128)(2,1)} %get-tuple-element.8.parts_ref) | copy-start | bytes 1966084
  35.6 1.0 %copy-start.2 = (f32[4,32,640]{2,1,0:T(8,128)S(1)}, f32[4,32,640]{2,1,0:T(8,128)}, u32[]{:S(2)}) copy-start(f32[4,32,640]{2,1,0:T(8,128)} %get-tuple-element.9.av_ref) | copy-start | bytes 983044

commit v5 on v4

--- a/solution.py
+++ b/solution.py
@@ -245,15 +245,17 @@
     core = lax.rem(dom, 2)
     sent = z_refs + z_last
     flying = [[]] + [[move] for move in z_refs] + [z_last]
-    for stage in range(bits):
-        for hop in range(groups + 1):
+    for tick in range(groups + bits):
+        for stage in reversed(range(bits)):
+            hop = tick - stage
+            if hop < 0 or hop > groups:
+                continue
             for move in flying[hop]:
                 move.wait_recv()
             if hop < groups:
-                source = lax.rem(cls + groups - hop, groups)
                 flying[hop] = begin(
                     stage,
-                    refs_piece(source),
+                    refs_piece(lax.rem(cls + groups - hop, groups)),
                     lambda half, spot: r_send.at[hop, half, spot],
                     lambda half, spot: r_recv.at[hop, half, spot],
                 )
@@ -265,21 +267,18 @@
                     lambda half, spot: f_recv.at[half, spot],
                 )
             sent.extend(flying[hop])
-            if stage == bits - 1:
-                for chunk in todo:
-                    roll_chunk(chunk)
-                todo = []
-                if hop < groups:
-                    multiply(source, core)
-            elif hop < groups:
-                for chunk in todo[: 2 if stage == hop == 0 else 1]:
-                    roll_chunk(chunk)
-                todo = todo[2 if stage == hop == 0 else 1 :]
-    for hop in range(groups + 1):
-        for move in flying[hop]:
-            move.wait_recv()
-        if hop < groups:
-            multiply(lax.rem(cls + groups - hop, groups), 1 - core)
+        for chunk in todo[:3]:
+            roll_chunk(chunk)
+        todo = todo[3:]
+        landed = tick - bits + 1
+        if 0 <= landed < groups:
+            multiply(lax.rem(cls + groups - landed, groups), core)
+        if 1 <= landed <= groups:
+            for move in flying[landed - 1]:
+                move.wait_recv()
+            multiply(lax.rem(cls + groups - landed + 1, groups), 1 - core)
+    for move in flying[groups]:
+        move.wait_recv()
 
     scale = 1.0 / math.sqrt(RADII * ANGLES)
     pack = ANGLES // per_group

time: 88.3 us -> 84.5 us (0.957)
  the two profiles are of different devices: /device:TPU:0 before, /device:TPU:27 now
where the time goes in v5:
time: 84.5 us; the launch traced here: 84.2 us
  Pallas kernels  73 us (86%)
  other arithmetic  6.54 us (8%)
  local copies, waits for them, and re-layouts  3.89 us (5%)
    pallas_call x1, Pallas kernels, per_device(): pl.pallas_call(functools.partial(gather_kernel, doms, groups), out_shape=...  42.6 us
    pallas_call x1, Pallas kernels, per_device(): pl.pallas_call(functools.partial(exchange_kernel, doms, groups), out_shap...  26.9 us
    pallas_call x1, Pallas kernels, per_device(): pl.pallas_call(update_kernel, out_shape=(jax.ShapeDtypeStruct((STEPS * pe...  3.53 us
    unnamed x12, local copies, waits for them, and re-layouts  2.87 us
    convert_element_type x1, other arithmetic, per_device(): return (scores, last.astype(jnp.float32))  2.68 us

profile of v5, /device:TPU:27, one launch (start us, length us, event | category | flops | bytes accessed | tf_op | source)
XLA Modules:
  0.0 84.2 jit_solution(258607939274188586)
XLA Ops:
  0.6 0.0 copy-start
  0.6 0.0 copy-start.4
  0.7 0.8 convert.12
  1.5 0.7 convert_bitcast_fusion
  2.2 0.7 pad_maximum_fusion.2
  2.9 0.1 copy.12
  3.0 0.7 broadcast_in_dim.8
  3.7 0.0 copy-done
  3.8 0.8 pad_maximum_fusion.1.band_ref
  4.6 0.0 copy-done.4
  4.6 0.0 copy-start.3
  4.6 0.1 fusion
  4.7 0.9 %pad_maximum_fusion.blocks_ref = bf16[32,80,128]{2,1,0:T(8,128)(2,1)} fusion(bf16[32,16,128]{2,1,0:T(8,128)(2,1)S(1)} %broadcast_in_dim.7, bf16[32,64,128]{2,1,0:T(8,128)(2,1)S(1)} %bitcast.28), kind=kLoop, calls=%fused_computation | loop fusion | flops 1310720 | bytes 1310720 | tf_op jit(solution)/shard_map/concatenate | solution.py:309
  5.6 26.9 %exchange.1 = (bf16[32,80,128]{2,1,0:T(8,128)(2,1)}, f32[4,32,640]{2,1,0:T(8,128)}) custom-call(bf16[32,80,128]{2,1,0:T(8,128)(2,1)} %pad_maximum_fusion.blocks_ref, f32[4,32,640]{2,1,0:T(8,128)} %pad_maximum_fusion.1.band_ref), custom_call_target="tpu_custom_call" | custom-call | tf_op jit(solution)/shard_map/exchange/pallas_call | solution.py:316
  32.5 0.0 copy-done.3
  32.5 0.0 copy-start.1
  32.5 1.1 %copy-done.1 = bf16[32,80,128]{2,1,0:T(8,128)(2,1)S(1)} copy-done((bf16[32,80,128]{2,1,0:T(8,128)(2,1)S(1)}, bf16[32,80,128]{2,1,0:T(8,128)(2,1)}, u32[]{:S(2)}) %copy-start.1) | copy-done | bytes 655384
  33.6 0.0 copy-start.2
  33.6 1.0 %copy-done.2 = f32[4,32,640]{2,1,0:T(8,128)S(1)} copy-done((f32[4,32,640]{2,1,0:T(8,128)S(1)}, f32[4,32,640]{2,1,0:T(8,128)}, u32[]{:S(2)}) %copy-start.2) | copy-done | bytes 327704
  34.5 3.5 %update.1 = (bf16[128,512]{1,0:T(8,128)(2,1)S(1)}, bf16[4,32,512]{2,1,0:T(8,128)(2,1)S(1)}) custom-call(s32[4]{0:T(128)S(1)} %copy-done.3, bf16[32,80,128]{2,1,0:T(8,128)(2,1)S(1)} %copy-done.1, f32[4,32,640]{2,1,0:T(8,128)S(1)} %copy-done.2), custom_call_target="tpu_custom_call" | custom-call | tf_op jit(solution)/shard_map/update/pallas_call | solution.py:326
  38.1 42.6 %gather_scores.1 = (bf16[32,16384]{1,0:T(8,128)(2,1)}, f32[4,16,2048]{2,1,0:T(8,128)S(1)}) custom-call(bf16[128,512]{1,0:T(8,128)(2,1)S(1)} %get-tuple-element.10.refs_ref, bf16[4,32,512]{2,1,0:T(8,128)(2,1)S(1)} %get-tuple-element.11.final_ref, bf16[128,16,128]{2,1,0:T(8,128)(2,1)S(1)} %get-tuple-element.14.images_ref), custom_call_target="tpu_custom_call" | custom-call | tf_op jit(solution)/shard_map/gather_scores/pallas_call | solution.py:339
  80.7 2.7 %convert_element_type.6 = f32[32,16384]{1,0:T(8,128)} convert(bf16[32,16384]{1,0:T(8,128)(2,1)} %get-tuple-element.13) | non-fusion elementwise | flops 524288 | bytes 3145728 | tf_op jit(solution)/shard_map/convert_element_type | solution.py:364
  83.4 0.8 copy.25
  (5 shorter events, 0.1 us)
Async XLA Ops:
  0.6 3.1 %copy-start = (f32[32,16384]{1,0:T(8,128)S(1)}, f32[32,16384]{1,0:T(8,128)}, u32[]{:S(2)}) copy-start(f32[32,16384]{1,0:T(8,128)} %param.9) | copy-start | bytes 6291460
  0.6 3.9 %copy-start.4 = (bf16[16,16384]{1,0:T(8,128)(2,1)S(1)}, bf16[16,16384]{1,0:T(8,128)(2,1)}, u32[]{:S(2)}) copy-start(bf16[16,16384]{1,0:T(8,128)(2,1)} %param.8) | copy-start | bytes 1572868
  4.6 27.9 %copy-start.3 = (s32[4]{0:T(128)S(1)}, s32[4]{0:T(128)}, u32[]{:S(2)}) copy-start(s32[4]{0:T(128)} %owners_ref.1) | copy-start | bytes 52
  32.5 1.1 %copy-start.1 = (bf16[32,80,128]{2,1,0:T(8,128)(2,1)S(1)}, bf16[32,80,128]{2,1,0:T(8,128)(2,1)}, u32[]{:S(2)}) copy-start(bf16[32,80,128]{2,1,0:T(8,128)(2,1)} %get-tuple-element.8.parts_ref) | copy-start | bytes 1966084
  33.6 1.0 %copy-start.2 = (f32[4,32,640]{2,1,0:T(8,128)S(1)}, f32[4,32,640]{2,1,0:T(8,128)}, u32[]{:S(2)}) copy-start(f32[4,32,640]{2,1,0:T(8,128)} %get-tuple-element.9.av_ref) | copy-start | bytes 983044

commit v6 on v5

--- a/solution.py
+++ b/solution.py
@@ -93,13 +93,13 @@
             pl.DeviceIdType.MESH,
         )
 
+    @pl.loop(1, groups)
+    def _(hop):
+        band(hop).start()
+
     @pl.loop(1, devices)
     def _(hop):
         block(hop).start()
-
-    @pl.loop(1, groups)
-    def _(hop):
-        band(hop).start()
 
     own = [
         pltpu.make_async_copy(blocks_ref.at[me], mine_ref.at[me], own_sem.at[0]),

time: 84.5 us -> 83.9 us (level)
  the two profiles are of different devices: /device:TPU:27 before, /device:TPU:0 now
where the time goes in v6:
time: 83.9 us; the launch traced here: 82.4 us
  Pallas kernels  71.3 us (85%)
  other arithmetic  6.54 us (8%)
  local copies, waits for them, and re-layouts  3.89 us (5%)
    pallas_call x1, Pallas kernels, per_device(): pl.pallas_call(functools.partial(gather_kernel, doms, groups), out_shape=...  37.6 us
    pallas_call x1, Pallas kernels, per_device(): pl.pallas_call(functools.partial(exchange_kernel, doms, groups), out_shap...  30.2 us
    pallas_call x1, Pallas kernels, per_device(): pl.pallas_call(update_kernel, out_shape=(jax.ShapeDtypeStruct((STEPS * pe...  3.52 us
    unnamed x12, local copies, waits for them, and re-layouts  2.87 us
    convert_element_type x1, other arithmetic, per_device(): return (scores, last.astype(jnp.float32))  2.68 us

profile of v6, /device:TPU:0, one launch (start us, length us, event | category | flops | bytes accessed | tf_op | source)
XLA Modules:
  0.0 82.4 jit_solution(10485790425536597835)
XLA Ops:
  0.6 0.0 copy-start
  0.6 0.0 copy-start.4
  0.7 0.8 %convert.12 = bf16[4,16,1]{1,2,0:T(2,128)(2,1)S(1)} convert(s32[4,16,1]{1,2,0:T(1,128)} %param.11) | non-fusion elementwise | flops 64 | bytes 384 | tf_op jit(solution)/shard_map/convert.5
  1.5 0.7 convert_bitcast_fusion
  2.2 0.7 pad_maximum_fusion.2
  2.9 0.1 copy.12
  3.0 0.7 broadcast_in_dim.8
  3.7 0.0 copy-done
  3.8 0.8 pad_maximum_fusion.1.band_ref
  4.6 0.0 copy-done.4
  4.6 0.0 copy-start.3
  4.6 0.1 fusion
  4.7 0.9 %pad_maximum_fusion.blocks_ref = bf16[32,80,128]{2,1,0:T(8,128)(2,1)} fusion(bf16[32,16,128]{2,1,0:T(8,128)(2,1)S(1)} %broadcast_in_dim.7, bf16[32,64,128]{2,1,0:T(8,128)(2,1)S(1)} %bitcast.28), kind=kLoop, calls=%fused_computation | loop fusion | flops 1310720 | bytes 1310720 | tf_op jit(solution)/shard_map/concatenate | solution.py:309
  5.6 30.2 %exchange.1 = (bf16[32,80,128]{2,1,0:T(8,128)(2,1)}, f32[4,32,640]{2,1,0:T(8,128)}) custom-call(bf16[32,80,128]{2,1,0:T(8,128)(2,1)} %pad_maximum_fusion.blocks_ref, f32[4,32,640]{2,1,0:T(8,128)} %pad_maximum_fusion.1.band_ref), custom_call_target="tpu_custom_call" | custom-call | tf_op jit(solution)/shard_map/exchange/pallas_call | solution.py:316
  35.8 0.0 copy-done.3
  35.8 0.0 copy-start.1
  35.8 1.1 %copy-done.1 = bf16[32,80,128]{2,1,0:T(8,128)(2,1)S(1)} copy-done((bf16[32,80,128]{2,1,0:T(8,128)(2,1)S(1)}, bf16[32,80,128]{2,1,0:T(8,128)(2,1)}, u32[]{:S(2)}) %copy-start.1) | copy-done | bytes 655384
  36.9 0.0 copy-start.2
  36.9 1.0 %copy-done.2 = f32[4,32,640]{2,1,0:T(8,128)S(1)} copy-done((f32[4,32,640]{2,1,0:T(8,128)S(1)}, f32[4,32,640]{2,1,0:T(8,128)}, u32[]{:S(2)}) %copy-start.2) | copy-done | bytes 327704
  37.9 3.5 %update.1 = (bf16[128,512]{1,0:T(8,128)(2,1)S(1)}, bf16[4,32,512]{2,1,0:T(8,128)(2,1)S(1)}) custom-call(s32[4]{0:T(128)S(1)} %copy-done.3, bf16[32,80,128]{2,1,0:T(8,128)(2,1)S(1)} %copy-done.1, f32[4,32,640]{2,1,0:T(8,128)S(1)} %copy-done.2), custom_call_target="tpu_custom_call" | custom-call | tf_op jit(solution)/shard_map/update/pallas_call | solution.py:326
  41.4 37.6 %gather_scores.1 = (bf16[32,16384]{1,0:T(8,128)(2,1)}, f32[4,16,2048]{2,1,0:T(8,128)S(1)}) custom-call(bf16[128,512]{1,0:T(8,128)(2,1)S(1)} %get-tuple-element.10.refs_ref, bf16[4,32,512]{2,1,0:T(8,128)(2,1)S(1)} %get-tuple-element.11.final_ref, bf16[128,16,128]{2,1,0:T(8,128)(2,1)S(1)} %get-tuple-element.14.images_ref), custom_call_target="tpu_custom_call" | custom-call | tf_op jit(solution)/shard_map/gather_scores/pallas_call | solution.py:339
  79.0 2.7 %convert_element_type.6 = f32[32,16384]{1,0:T(8,128)} convert(bf16[32,16384]{1,0:T(8,128)(2,1)} %get-tuple-element.13) | non-fusion elementwise | flops 524288 | bytes 3145728 | tf_op jit(solution)/shard_map/convert_element_type | solution.py:364
  81.7 0.8 copy.25
  (5 shorter events, 0.1 us)
Async XLA Ops:
  0.6 3.1 %copy-start = (f32[32,16384]{1,0:T(8,128)S(1)}, f32[32,16384]{1,0:T(8,128)}, u32[]{:S(2)}) copy-start(f32[32,16384]{1,0:T(8,128)} %param.9) | copy-start | bytes 6291460
  0.6 3.9 %copy-start.4 = (bf16[16,16384]{1,0:T(8,128)(2,1)S(1)}, bf16[16,16384]{1,0:T(8,128)(2,1)}, u32[]{:S(2)}) copy-start(bf16[16,16384]{1,0:T(8,128)(2,1)} %param.8) | copy-start | bytes 1572868
  4.6 31.2 %copy-start.3 = (s32[4]{0:T(128)S(1)}, s32[4]{0:T(128)}, u32[]{:S(2)}) copy-start(s32[4]{0:T(128)} %owners_ref.1) | copy-start | bytes 52
  35.8 1.1 %copy-start.1 = (bf16[32,80,128]{2,1,0:T(8,128)(2,1)S(1)}, bf16[32,80,128]{2,1,0:T(8,128)(2,1)}, u32[]{:S(2)}) copy-start(bf16[32,80,128]{2,1,0:T(8,128)(2,1)} %get-tuple-element.8.parts_ref) | copy-start | bytes 1966084
  36.9 1.0 %copy-start.2 = (f32[4,32,640]{2,1,0:T(8,128)S(1)}, f32[4,32,640]{2,1,0:T(8,128)}, u32[]{:S(2)}) copy-start(f32[4,32,640]{2,1,0:T(8,128)} %get-tuple-element.9.av_ref) | copy-start | bytes 983044

commit v7 on v6

--- a/solution.py
+++ b/solution.py
@@ -231,13 +231,15 @@
             rolled[part, r * per_dev : (r + 1) * per_dev, :] = turned.reshape(depth, per_dev, ANGLES)
 
     def multiply(source, core):
-        @pl.loop(0, doms // 2)
+        @pl.loop(0, doms // 4)
         def _(pair):
-            which = 2 * pair + core
-            base = (which * groups + source) * radii
-            views = jnp.concatenate([rolled[base + j] for j in range(radii)], axis=1)
+            picks = [4 * pair + core, 4 * pair + 2 + core]
+            views = jnp.concatenate(
+                [rolled[(which * groups + source) * radii + j] for which in picks for j in range(radii)], axis=1
+            )
+            names = jnp.concatenate([slots_ref[which, source] for which in picks], axis=1)
             total[...] += lax.dot_general(
-                views, slots_ref[which, source], (((1,), (1,)), ((), ())), preferred_element_type=jnp.float32
+                views, names, (((1,), (1,)), ((), ())), preferred_element_type=jnp.float32
             )
 
     total[...] = jnp.zeros_like(total)

time: 83.9 us -> 83.6 us (level)
  no operation moved by 1% of the time
where the time goes in v7:
time: 83.6 us; the launch traced here: 82 us
  Pallas kernels  70.8 us (85%)
  other arithmetic  6.54 us (8%)
  local copies, waits for them, and re-layouts  3.89 us (5%)
    pallas_call x1, Pallas kernels, per_device(): pl.pallas_call(functools.partial(gather_kernel, doms, groups), out_shape=...  37.1 us
    pallas_call x1, Pallas kernels, per_device(): pl.pallas_call(functools.partial(exchange_kernel, doms, groups), out_shap...  30.2 us
    pallas_call x1, Pallas kernels, per_device(): pl.pallas_call(update_kernel, out_shape=(jax.ShapeDtypeStruct((STEPS * pe...  3.52 us
    unnamed x12, local copies, waits for them, and re-layouts  2.87 us
    convert_element_type x1, other arithmetic, per_device(): return (scores, last.astype(jnp.float32))  2.68 us

profile of v7, /device:TPU:0, one launch (start us, length us, event | category | flops | bytes accessed | tf_op | source)
XLA Modules:
  0.0 82.0 jit_solution(4416812728229259634)
XLA Ops:
  0.6 0.0 copy-start
  0.6 0.0 copy-start.4
  0.7 0.8 %convert.12 = bf16[4,16,1]{1,2,0:T(2,128)(2,1)S(1)} convert(s32[4,16,1]{1,2,0:T(1,128)} %param.11) | non-fusion elementwise | flops 64 | bytes 384 | tf_op jit(solution)/shard_map/convert.5
  1.5 0.7 convert_bitcast_fusion
  2.2 0.7 pad_maximum_fusion.2
  2.9 0.1 copy.12
  3.0 0.7 broadcast_in_dim.8
  3.7 0.0 copy-done
  3.8 0.8 pad_maximum_fusion.1.band_ref
  4.6 0.0 copy-done.4
  4.6 0.0 copy-start.3
  4.6 0.1 fusion
  4.7 0.9 %pad_maximum_fusion.blocks_ref = bf16[32,80,128]{2,1,0:T(8,128)(2,1)} fusion(bf16[32,16,128]{2,1,0:T(8,128)(2,1)S(1)} %broadcast_in_dim.7, bf16[32,64,128]{2,1,0:T(8,128)(2,1)S(1)} %bitcast.28), kind=kLoop, calls=%fused_computation | loop fusion | flops 1310720 | bytes 1310720 | tf_op jit(solution)/shard_map/concatenate | solution.py:311
  5.6 30.2 %exchange.1 = (bf16[32,80,128]{2,1,0:T(8,128)(2,1)}, f32[4,32,640]{2,1,0:T(8,128)}) custom-call(bf16[32,80,128]{2,1,0:T(8,128)(2,1)} %pad_maximum_fusion.blocks_ref, f32[4,32,640]{2,1,0:T(8,128)} %pad_maximum_fusion.1.band_ref), custom_call_target="tpu_custom_call" | custom-call | tf_op jit(solution)/shard_map/exchange/pallas_call | solution.py:318
  35.8 0.0 copy-done.3
  35.8 0.0 copy-start.1
  35.8 1.1 %copy-done.1 = bf16[32,80,128]{2,1,0:T(8,128)(2,1)S(1)} copy-done((bf16[32,80,128]{2,1,0:T(8,128)(2,1)S(1)}, bf16[32,80,128]{2,1,0:T(8,128)(2,1)}, u32[]{:S(2)}) %copy-start.1) | copy-done | bytes 655384
  36.9 0.0 copy-start.2
  36.9 1.0 %copy-done.2 = f32[4,32,640]{2,1,0:T(8,128)S(1)} copy-done((f32[4,32,640]{2,1,0:T(8,128)S(1)}, f32[4,32,640]{2,1,0:T(8,128)}, u32[]{:S(2)}) %copy-start.2) | copy-done | bytes 327704
  37.9 3.5 %update.1 = (bf16[128,512]{1,0:T(8,128)(2,1)S(1)}, bf16[4,32,512]{2,1,0:T(8,128)(2,1)S(1)}) custom-call(s32[4]{0:T(128)S(1)} %copy-done.3, bf16[32,80,128]{2,1,0:T(8,128)(2,1)S(1)} %copy-done.1, f32[4,32,640]{2,1,0:T(8,128)S(1)} %copy-done.2), custom_call_target="tpu_custom_call" | custom-call | tf_op jit(solution)/shard_map/update/pallas_call | solution.py:328
  41.4 37.1 %gather_scores.1 = (bf16[32,16384]{1,0:T(8,128)(2,1)}, f32[4,16,2048]{2,1,0:T(8,128)S(1)}) custom-call(bf16[128,512]{1,0:T(8,128)(2,1)S(1)} %get-tuple-element.10.refs_ref, bf16[4,32,512]{2,1,0:T(8,128)(2,1)S(1)} %get-tuple-element.11.final_ref, bf16[128,16,128]{2,1,0:T(8,128)(2,1)S(1)} %get-tuple-element.14.images_ref), custom_call_target="tpu_custom_call" | custom-call | tf_op jit(solution)/shard_map/gather_scores/pallas_call | solution.py:341
  78.5 2.7 %convert_element_type.6 = f32[32,16384]{1,0:T(8,128)} convert(bf16[32,16384]{1,0:T(8,128)(2,1)} %get-tuple-element.13) | non-fusion elementwise | flops 524288 | bytes 3145728 | tf_op jit(solution)/shard_map/convert_element_type | solution.py:366
  81.2 0.8 copy.25
  (5 shorter events, 0.1 us)
Async XLA Ops:
  0.6 3.1 %copy-start = (f32[32,16384]{1,0:T(8,128)S(1)}, f32[32,16384]{1,0:T(8,128)}, u32[]{:S(2)}) copy-start(f32[32,16384]{1,0:T(8,128)} %param.9) | copy-start | bytes 6291460
  0.6 3.9 %copy-start.4 = (bf16[16,16384]{1,0:T(8,128)(2,1)S(1)}, bf16[16,16384]{1,0:T(8,128)(2,1)}, u32[]{:S(2)}) copy-start(bf16[16,16384]{1,0:T(8,128)(2,1)} %param.8) | copy-start | bytes 1572868
  4.6 31.2 %copy-start.3 = (s32[4]{0:T(128)S(1)}, s32[4]{0:T(128)}, u32[]{:S(2)}) copy-start(s32[4]{0:T(128)} %owners_ref.1) | copy-start | bytes 52
  35.8 1.1 %copy-start.1 = (bf16[32,80,128]{2,1,0:T(8,128)(2,1)S(1)}, bf16[32,80,128]{2,1,0:T(8,128)(2,1)}, u32[]{:S(2)}) copy-start(bf16[32,80,128]{2,1,0:T(8,128)(2,1)} %get-tuple-element.8.parts_ref) | copy-start | bytes 1966084
  36.9 1.0 %copy-start.2 = (f32[4,32,640]{2,1,0:T(8,128)S(1)}, f32[4,32,640]{2,1,0:T(8,128)}, u32[]{:S(2)}) copy-start(f32[4,32,640]{2,1,0:T(8,128)} %get-tuple-element.9.av_ref) | copy-start | bytes 983044
